TPU v7x, 32 devices: a whole 2x2x4 slice. The times are simulated.
32 devices in a mesh: shard: 4 (over z), heads: 4 (over x, core), tensor: 2 (over y).
Axes of the slice: x: 2, y: 2, z: 4, core: 2. Of those that a mesh axis runs over, the one named last changes fastest.
Arguments:
- tokens: bfloat16 [4096, 1088], P(('shard', 'heads', 'tensor')), may hold values from -6 to 6
- cotangent: bfloat16 [4096, 1088], P(('shard', 'heads')), may hold values from -6 to 6
- cut_pos: int32 [4], replicated, may hold values from 768 to 1023, as said below
- attend_weight: bfloat16 [1088, 3264], P(('shard', 'tensor')), may hold values from -0.1875 to 0.1875
- out_weight: bfloat16 [1088, 1088], P(('shard', 'tensor')), may hold values from -3 to 3
- up_weight: bfloat16 [1088, 4352], P(None, ('shard', 'tensor')), may hold values from -0.1875 to 0.1875
- down_weight: bfloat16 [4352, 1088], P(('shard', 'tensor')), may hold values from -0.09375 to 0.09375
- first_gain: bfloat16 [1088], P(('shard', 'tensor')), may hold values from 0.5 to 1.5
- first_bias: bfloat16 [1088], P(('shard', 'tensor')), may hold values from -1.5 to 1.5
- query_bias: bfloat16 [1088], P(('shard', 'tensor')), may hold values from -1.5 to 1.5
- value_bias: bfloat16 [1088], P(('shard', 'tensor')), may hold values from -1.5 to 1.5
- out_bias: bfloat16 [1088], P(('shard', 'tensor')), may hold values from -1.5 to 1.5
- second_gain: bfloat16 [1088], P(('shard', 'tensor')), may hold values from 0.5 to 1.5
- second_bias: bfloat16 [1088], P(('shard', 'tensor')), may hold values from -1.5 to 1.5
- up_bias: bfloat16 [4352], P(('shard', 'tensor')), may hold values from -1.5 to 1.5
- down_bias: bfloat16 [1088], P(('shard', 'tensor')), may hold values from -1.5 to 1.5
Outputs:
- layer_out: bfloat16 [4096, 1088], P(('shard', 'heads', 'tensor'))
- tokens_grad: float32 [4096, 1088], P(('shard', 'heads', 'tensor'))
- attend_weight_grad: float32 [1088, 3264], P(('shard', 'tensor'))
- out_weight_grad: float32 [1088, 1088], P(('shard', 'tensor'))
- up_weight_grad: float32 [1088, 4352], P(None, ('shard', 'tensor'))
- down_weight_grad: float32 [4352, 1088], P(('shard', 'tensor'))
- first_gain_grad: float32 [1088], P(('shard', 'tensor'))
- first_bias_grad: float32 [1088], P(('shard', 'tensor'))
- query_bias_grad: float32 [1088], P(('shard', 'tensor'))
- value_bias_grad: float32 [1088], P(('shard', 'tensor'))
- out_bias_grad: float32 [1088], P(('shard', 'tensor'))
- second_gain_grad: float32 [1088], P(('shard', 'tensor'))
- second_bias_grad: float32 [1088], P(('shard', 'tensor'))
- up_bias_grad: float32 [4352], P(('shard', 'tensor'))
- down_bias_grad: float32 [1088], P(('shard', 'tensor'))
Inputs may be any that keep to these rules, and one draw needn't show every extreme that they name: cut_pos[s] is the offset within the 1024 tokens of group s at which a new sequence begins; every other token continues the sequence of the token before it, and the very first token begins one. So no sequence spans more than two groups.
All inputs are finite; a program needn't handle non-finite values.
Results may differ from a plain program's by a relative error of at most 0.015.
Values may be sent and summed in bfloat16 or wider, within the bound.
A program may use at most 192 MiB of HBM per device.

v0:
```python
import jax
import jax.numpy as jnp
import numpy as np
from jax import lax
from jax.sharding import PartitionSpec as P

NH = 17
HD = 64
SLOTS = 3


EPS = 1e-05
NEG = -1e30


def from_behind(value, axis, steps):
    count = lax.axis_size(axis)
    leading, last = (max(0, -steps), min(count, count - steps))
    return lax.ppermute(value, axis, [(source, source + steps) for source in range(leading, last)])


def layer_norm(values, gain_vec, shift_vec):
    center = values - jnp.mean(values, axis=-1, keepdims=True)
    spread = jnp.mean(center * center, axis=-1, keepdims=True)
    return center * lax.rsqrt(spread + EPS) * gain_vec + shift_vec


def gelu_tanh(values):
    return jax.nn.gelu(values, approximate=True)


def slot_entries(group_total, tensor_total, per_device):
    base_count = NH // group_total
    extra_count = NH % group_total
    entry_list = []
    next_head = 0
    for group_idx in range(group_total):
        group_size = base_count + (1 if group_idx < extra_count else 0)
        larger = group_size - group_size // 2
        for tensor_pos in range(tensor_total):
            filled = larger if tensor_pos == 0 else group_size - larger
            for slot_idx in range(per_device):
                if slot_idx < filled:
                    entry_list.append(next_head)
                    next_head = next_head + 1
                else:
                    entry_list.append(NH)
    return np.array(entry_list, dtype=np.int32)


def to_heads(values):
    return lax.all_to_all(values, ("heads", "tensor"), split_axis=2, concat_axis=0, tiled=True)


def to_tokens(values):
    return lax.all_to_all(values, ("heads", "tensor"), split_axis=0, concat_axis=2, tiled=True)


def unit_sums(values):
    return lax.psum_scatter(
        values.astype(jnp.bfloat16), "tensor", scatter_dimension=0, tiled=True
    ).astype(jnp.float32)


def shards(
    tokens,
    cotangent,
    cut_pos,
    attend_weight,
    out_weight,
    up_weight,
    down_weight,
    first_gain,
    first_bias,
    query_bias,
    value_bias,
    out_bias,
    second_gain,
    second_bias,
    up_bias,
    down_bias,
):
    tok_rows = tokens.shape[0]
    model_width = tokens.shape[1]
    heads_count = lax.axis_size("heads")
    tensor_count = lax.axis_size("tensor")
    group_devices = heads_count * tensor_count
    group_tok = tok_rows * group_devices
    prev_tok = group_tok // 4
    key_count = group_tok + prev_tok
    query_block = min(512, group_tok)
    block_count = group_tok // query_block
    score_scale = HD ** (-0.5)
    slot_width = SLOTS * HD
    shard_idx = lax.axis_index("shard")
    tensor_idx = lax.axis_index("tensor")
    entries = slot_entries(heads_count, tensor_count, SLOTS)
    valid_slot = jnp.asarray(entries < NH).astype(jnp.bfloat16)
    source_head = jnp.asarray(np.minimum(entries, NH - 1))
    head_place = jnp.asarray(
        np.array([list(entries).index(head_id) for head_id in range(NH)], dtype=np.int32)
    )
    (
        w_attend,
        w_out,
        gain_one,
        shift_one,
        bias_query,
        bias_value,
        bias_out,
        gain_two,
        shift_two,
        bias_down,
    ) = (
        lax.all_gather(attend_weight, ("shard", "tensor"), axis=0, tiled=True),
        lax.all_gather(out_weight, ("shard", "tensor"), axis=0, tiled=True),
        lax.all_gather(first_gain, ("shard", "tensor"), axis=0, tiled=True),
        lax.all_gather(first_bias, ("shard", "tensor"), axis=0, tiled=True),
        lax.all_gather(query_bias, ("shard", "tensor"), axis=0, tiled=True),
        lax.all_gather(value_bias, ("shard", "tensor"), axis=0, tiled=True),
        lax.all_gather(out_bias, ("shard", "tensor"), axis=0, tiled=True),
        lax.all_gather(second_gain, ("shard", "tensor"), axis=0, tiled=True),
        lax.all_gather(second_bias, ("shard", "tensor"), axis=0, tiled=True),
        lax.all_gather(down_bias, ("shard", "tensor"), axis=0, tiled=True),
    )
    token_f = tokens.astype(jnp.float32)
    normed_f, norm_one_back = jax.vjp(
        layer_norm, token_f, gain_one.astype(jnp.float32), shift_one.astype(jnp.float32)
    )
    normed = normed_f.astype(jnp.bfloat16)
    bias_all = jnp.concatenate(
        [
            bias_query.astype(jnp.float32),
            jnp.zeros((model_width,), jnp.float32),
            bias_value.astype(jnp.float32),
        ]
    )
    projected_f = jnp.dot(normed, w_attend, preferred_element_type=jnp.float32)
    projected = (projected_f + bias_all).astype(jnp.bfloat16)
    per_head = projected.reshape(tok_rows, 3, NH, HD)
    slotted = jnp.take(per_head, source_head, axis=2) * valid_slot[None, None, :, None]
    arrived = to_heads(slotted.reshape(tok_rows, 3, group_devices, slot_width))
    query_rows = arrived[:, 0, 0].reshape(group_tok, SLOTS, HD)
    tail_rows = arrived[group_tok - prev_tok :, 1:3, 0]
    earlier = from_behind(tail_rows, "shard", 1)
    key_rows = jnp.concatenate([earlier[:, 0], arrived[:, 1, 0]], axis=0).reshape(
        key_count, SLOTS, HD
    )
    value_rows = jnp.concatenate([earlier[:, 1], arrived[:, 2, 0]], axis=0).reshape(
        key_count, SLOTS, HD
    )
    cut_here = cut_pos[shard_idx]
    cut_before = cut_pos[jnp.maximum(shard_idx - 1, 0)]
    earlier_start = jnp.where(shard_idx > 0, cut_before - group_tok, 0)
    local_query = jnp.arange(group_tok, dtype=jnp.int32)
    seq_start = jnp.where(local_query >= cut_here, cut_here, earlier_start)
    local_key = jnp.arange(key_count, dtype=jnp.int32) - prev_tok
    query_blocks = query_rows.reshape(block_count, query_block, SLOTS, HD)
    position_blocks = local_query.reshape(block_count, query_block)
    start_blocks = seq_start.reshape(block_count, query_block)

    def block_scores(query_part, position_part, start_part):
        scores = (
            jnp.einsum("qhd,khd->hqk", query_part, key_rows, preferred_element_type=jnp.float32)
            * score_scale
        )
        allowed = (local_key[None, :] >= start_part[:, None]) & (
            local_key[None, :] <= position_part[:, None]
        )
        return jnp.where(allowed[None], scores, NEG)

    def attend(block_items):
        query_part, position_part, start_part = block_items
        scores = block_scores(query_part, position_part, start_part)
        row_max = jnp.max(scores, axis=-1, keepdims=True)
        exp_scores = jnp.exp(scores - row_max)
        row_total = jnp.sum(exp_scores, axis=-1, keepdims=True)
        weights = (exp_scores / row_total).astype(jnp.bfloat16)
        result = jnp.einsum("hqk,khd->qhd", weights, value_rows, preferred_element_type=jnp.float32)
        return (result.astype(jnp.bfloat16), (row_max + jnp.log(row_total))[..., 0])

    attended, log_totals = lax.map(attend, (query_blocks, position_blocks, start_blocks))
    returned = to_tokens(attended.reshape(group_tok, 1, 1, slot_width)).reshape(
        tok_rows, group_devices * SLOTS, HD
    )
    attn_tok = jnp.take(returned, head_place, axis=1).reshape(tok_rows, model_width)
    branch_f = jnp.dot(attn_tok, w_out, preferred_element_type=jnp.float32)
    resid = token_f + branch_f + bias_out.astype(jnp.float32)
    normed_two_f, norm_two_back = jax.vjp(
        layer_norm, resid, gain_two.astype(jnp.float32), shift_two.astype(jnp.float32)
    )
    normed_two = normed_two_f.astype(jnp.bfloat16)
    own_grad_rows = lax.dynamic_slice_in_dim(cotangent, tensor_idx * tok_rows, tok_rows, 0)
    w_up, w_down, bias_up = (
        lax.all_gather(up_weight, "shard", axis=1, tiled=True),
        lax.all_gather(down_weight, "shard", axis=0, tiled=True),
        lax.all_gather(up_bias, "shard", axis=0, tiled=True),
    )
    mlp_rows = lax.all_gather(normed_two, "tensor", axis=0, tiled=True)
    hidden_pre = jnp.dot(mlp_rows, w_up, preferred_element_type=jnp.float32) + bias_up.astype(
        jnp.float32
    )
    hidden_act_f, gelu_back = jax.vjp(gelu_tanh, hidden_pre)
    hidden_act = hidden_act_f.astype(jnp.bfloat16)
    partial_out = jnp.dot(hidden_act, w_down, preferred_element_type=jnp.float32)
    fed_rows = unit_sums(partial_out)
    layer_out = (resid + fed_rows + bias_down.astype(jnp.float32)).astype(jnp.bfloat16)
    d_act = jnp.dot(cotangent, w_down.T, preferred_element_type=jnp.float32)
    (d_pre_f,) = gelu_back(d_act)
    d_pre = d_pre_f.astype(jnp.bfloat16)
    g_down = jnp.dot(hidden_act.T, cotangent, preferred_element_type=jnp.float32)
    g_up = jnp.dot(mlp_rows.T, d_pre, preferred_element_type=jnp.float32)
    g_bias_up = jnp.sum(d_pre.astype(jnp.float32), axis=0)
    d_normed_two = jnp.dot(d_pre, w_up.T, preferred_element_type=jnp.float32)
    d_normed_two = unit_sums(d_normed_two)
    g_up_part, g_down_part, g_bias_up_part = (
        lax.psum_scatter(
            g_up.astype(jnp.bfloat16), "shard", scatter_dimension=1, tiled=True
        ).astype(jnp.float32),
        lax.psum_scatter(
            g_down.astype(jnp.bfloat16), "shard", scatter_dimension=0, tiled=True
        ).astype(jnp.float32),
        lax.psum_scatter(
            g_bias_up.astype(jnp.bfloat16), "shard", scatter_dimension=0, tiled=True
        ).astype(jnp.float32),
    )
    own_grad_f = own_grad_rows.astype(jnp.float32)
    g_bias_down = jnp.sum(own_grad_f, axis=0)
    d_resid_norm, g_gain_two, g_shift_two = norm_two_back(d_normed_two)
    d_resid = own_grad_f + d_resid_norm
    d_branch = d_resid.astype(jnp.bfloat16)
    g_bias_out = jnp.sum(d_branch.astype(jnp.float32), axis=0)
    g_out = jnp.dot(attn_tok.T, d_branch, preferred_element_type=jnp.float32)
    d_attended = jnp.dot(d_branch, w_out.T, preferred_element_type=jnp.float32).astype(jnp.bfloat16)
    d_slotted = (
        jnp.take(d_attended.reshape(tok_rows, NH, HD), source_head, axis=1)
        * valid_slot[None, :, None]
    )
    d_arrived = to_heads(d_slotted.reshape(tok_rows, 1, group_devices, slot_width))
    d_result = d_arrived[:, 0, 0].reshape(block_count, query_block, SLOTS, HD)

    def attend_back(grad_carry, block_items):
        key_grad, value_grad = grad_carry
        query_part, position_part, start_part, d_part, log_part = block_items
        scores = block_scores(query_part, position_part, start_part)
        probs_f = jnp.exp(scores - log_part[..., None])
        d_probs = jnp.einsum("qhd,khd->hqk", d_part, value_rows, preferred_element_type=jnp.float32)
        row_inner = jnp.sum(probs_f * d_probs, axis=-1, keepdims=True)
        d_scores = (probs_f * (d_probs - row_inner)).astype(jnp.bfloat16)
        query_grad = (
            jnp.einsum("hqk,khd->qhd", d_scores, key_rows, preferred_element_type=jnp.float32)
            * score_scale
        )
        key_grad = (
            key_grad
            + jnp.einsum("hqk,qhd->khd", d_scores, query_part, preferred_element_type=jnp.float32)
            * score_scale
        )
        value_grad = value_grad + jnp.einsum(
            "hqk,qhd->khd", probs_f.astype(jnp.bfloat16), d_part, preferred_element_type=jnp.float32
        )
        return ((key_grad, value_grad), query_grad)

    zero_keys = jnp.zeros((key_count, SLOTS, HD), jnp.float32)
    (key_grad, value_grad), query_grad = lax.scan(
        attend_back,
        (zero_keys, zero_keys),
        (query_blocks, position_blocks, start_blocks, d_result, log_totals),
    )
    spill_rows = jnp.stack(
        [
            key_grad[:prev_tok].reshape(prev_tok, slot_width),
            value_grad[:prev_tok].reshape(prev_tok, slot_width),
        ],
        axis=1,
    )
    later_rows = from_behind(spill_rows.astype(jnp.bfloat16), "shard", -1).astype(spill_rows.dtype)
    own_keys = (
        key_grad[prev_tok:]
        .reshape(group_tok, slot_width)
        .at[group_tok - prev_tok :]
        .add(later_rows[:, 0])
    )
    own_values = (
        value_grad[prev_tok:]
        .reshape(group_tok, slot_width)
        .at[group_tok - prev_tok :]
        .add(later_rows[:, 1])
    )
    d_heads = jnp.stack(
        [query_grad.reshape(group_tok, slot_width), own_keys, own_values], axis=1
    ).astype(jnp.bfloat16)[:, :, None, :]
    d_back = to_tokens(d_heads).reshape(tok_rows, 3, group_devices * SLOTS, HD)
    d_projected = jnp.take(d_back, head_place, axis=2).reshape(tok_rows, 3 * model_width)
    d_projected_f = d_projected.astype(jnp.float32)
    g_bias_query = jnp.sum(d_projected_f[:, :model_width], axis=0)
    g_bias_value = jnp.sum(d_projected_f[:, 2 * model_width :], axis=0)
    g_attend = jnp.dot(normed.T, d_projected, preferred_element_type=jnp.float32)
    d_normed = jnp.dot(d_projected, w_attend.T, preferred_element_type=jnp.float32)
    d_token_norm, g_gain_one, g_shift_one = norm_one_back(d_normed)
    tokens_grad = d_resid + d_token_norm
    reduced = (
        lax.psum_scatter(g_attend, ("shard", "tensor"), scatter_dimension=0, tiled=True),
        lax.psum_scatter(g_out, ("shard", "tensor"), scatter_dimension=0, tiled=True),
        lax.psum_scatter(g_gain_one, ("shard", "tensor"), scatter_dimension=0, tiled=True),
        lax.psum_scatter(g_shift_one, ("shard", "tensor"), scatter_dimension=0, tiled=True),
        lax.psum_scatter(g_bias_query, ("shard", "tensor"), scatter_dimension=0, tiled=True),
        lax.psum_scatter(g_bias_value, ("shard", "tensor"), scatter_dimension=0, tiled=True),
        lax.psum_scatter(g_bias_out, ("shard", "tensor"), scatter_dimension=0, tiled=True),
        lax.psum_scatter(g_gain_two, ("shard", "tensor"), scatter_dimension=0, tiled=True),
        lax.psum_scatter(g_shift_two, ("shard", "tensor"), scatter_dimension=0, tiled=True),
        lax.psum_scatter(g_bias_down, ("shard", "tensor"), scatter_dimension=0, tiled=True),
    )
    s_attend = reduced[0]
    s_out = reduced[1]
    small_list = [reduced[member + 2] for member in range(8)]
    summed = (
        lax.psum(s_attend.astype(jnp.bfloat16), "heads").astype(jnp.float32),
        lax.psum(s_out.astype(jnp.bfloat16), "heads").astype(jnp.float32),
        lax.psum(g_up_part.astype(jnp.bfloat16), "heads").astype(jnp.float32),
        lax.psum(g_down_part.astype(jnp.bfloat16), "heads").astype(jnp.float32),
        lax.psum(small_list[0].astype(jnp.bfloat16), "heads").astype(jnp.float32),
        lax.psum(small_list[1].astype(jnp.bfloat16), "heads").astype(jnp.float32),
        lax.psum(small_list[2].astype(jnp.bfloat16), "heads").astype(jnp.float32),
        lax.psum(small_list[3].astype(jnp.bfloat16), "heads").astype(jnp.float32),
        lax.psum(small_list[4].astype(jnp.bfloat16), "heads").astype(jnp.float32),
        lax.psum(small_list[5].astype(jnp.bfloat16), "heads").astype(jnp.float32),
        lax.psum(small_list[6].astype(jnp.bfloat16), "heads").astype(jnp.float32),
        lax.psum(g_bias_up_part.astype(jnp.bfloat16), "heads").astype(jnp.float32),
        lax.psum(small_list[7].astype(jnp.bfloat16), "heads").astype(jnp.float32),
    )
    return (
        layer_out,
        tokens_grad,
        summed[0],
        summed[1],
        summed[2],
        summed[3],
        summed[4],
        summed[5],
        summed[6],
        summed[7],
        summed[8],
        summed[9],
        summed[10],
        summed[11],
        summed[12],
    )


def solution(mesh):
    placed = (
        P(("shard", "heads", "tensor"), None),
        P(("shard", "heads"), None),
        P(),
        P(("shard", "tensor"), None),
        P(("shard", "tensor"), None),
        P(None, ("shard", "tensor")),
        P(("shard", "tensor"), None),
        P(("shard", "tensor")),
        P(("shard", "tensor")),
        P(("shard", "tensor")),
        P(("shard", "tensor")),
        P(("shard", "tensor")),
        P(("shard", "tensor")),
        P(("shard", "tensor")),
        P(("shard", "tensor")),
        P(("shard", "tensor")),
    )
    return jax.shard_map(
        shards,
        mesh=mesh,
        in_specs=placed,
        out_specs=(
            P(("shard", "heads", "tensor"), None),
            P(("shard", "heads", "tensor"), None),
            P(("shard", "tensor"), None),
            P(("shard", "tensor"), None),
            P(None, ("shard", "tensor")),
            P(("shard", "tensor"), None),
            P(("shard", "tensor")),
            P(("shard", "tensor")),
            P(("shard", "tensor")),
            P(("shard", "tensor")),
            P(("shard", "tensor")),
            P(("shard", "tensor")),
            P(("shard", "tensor")),
            P(("shard", "tensor")),
            P(("shard", "tensor")),
        ),
        check_vma=False,
    )
```

profile of v0, /device:TPU:0, one launch (start us, length us, event | category | flops | bytes accessed | tf_op | source)
XLA Modules:
  0.0 1062.3 jit_solution(16754429843619418704)
XLA Ops:
  12.9 40.1 %all-reduce.20 = (bf16[1088]{0:T(1024)(128)(2,1)S(1)}, bf16[1088]{0:T(1024)(128)(2,1)S(1)}, bf16[1088]{0:T(1024)(128)(2,1)S(1)}, bf16[1088]{0:T(1024)(128)(2,1)S...) all-reduce(bf16[1088]{0:T(1024)(128)(2,1)S(1)} %dynamic-update-slic, ...), channel_id=1, replica_groups=mesh['shard'=4,'heads'=4,'tensor'=2] {'shard','tensor'}, use_global_device_ids=true, to_apply=%add.2 | all-reduce | flops 8704 | bytes 34816
  53.7 70.8 %all-gather.5.cloned.1.call-done = bf16[1088,3264]{1,0:T(8,128)(2,1)} async-done(((bf16[136,3264]{1,0:T(8,128)(2,1)}), bf16[1088,3264]{1,0:T(8,128)(2,1)}) %all-gather.5.cloned.1.call-update) | async-done | bytes 7102480 | tf_op jit(solution)/shard_map/all_gather | solution.py:115
  124.5 6.4 fusion.41
  138.5 10.5 all-reduce.7
  155.6 8.3 collective-permute-done
  163.9 14.5 %while.32 = (s32[]{:T(128)}, bf16[2,512,3,64]{1,3,2,0:T(8,128)(2,1)S(1)}, f32[2,3,512]{2,1,0:T(4,128)S(1)}, s32[2,512]{1,0:T(2,128)S(1)}, s32[2,512]{1,0:T(2,128...) while((s32[]{:T(128)}, ...), condition=%wide.region_5.6_spmd.clone.clone, body=%wide.region_2.5_spmd.clone.clone.sunk | while | flops 528973568 | bytes 27672692 | solution.py:182
  185.6 33.7 %all-gather.11.cloned.1.call-done = bf16[2176,1088]{1,0:T(8,128)(2,1)} async-done(((bf16[544,1088]{1,0:T(8,128)(2,1)}), bf16[2176,1088]{1,0:T(8,128)(2,1)}) %all-gather.11.cloned.1.call-update) | async-done | bytes 4734992 | tf_op jit(solution)/shard_map/all_gather | solution.py:196
  219.2 5.7 fusion.87
  227.1 50.1 %all-gather.7.cloned.1.call-done = bf16[1088,1088]{1,0:T(8,128)(2,1)} async-done(((bf16[136,1088]{1,0:T(8,128)(2,1)}), bf16[1088,1088]{1,0:T(8,128)(2,1)}) %all-gather.7.cloned.1.call-update) | async-done | bytes 2367504 | tf_op jit(solution)/shard_map/all_gather | solution.py:116
  280.6 8.0 all_gather.51
  288.7 82.8 %all-gather.9.cloned.1.call-done = bf16[1088,2176]{0,1:T(8,128)(2,1)} async-done(((bf16[1088,544]{0,1:T(8,128)(2,1)}), bf16[1088,2176]{0,1:T(8,128)(2,1)}) %all-gather.9.cloned.1.call-update) | async-done | bytes 4734992 | tf_op jit(solution)/shard_map/all_gather | solution.py:195
  371.5 7.6 fusion.78
  383.3 13.8 %reduce-scatter.21.cloned.1.call-done = bf16[128,1088]{1,0:T(8,128)(2,1)} async-done(((bf16[256,1088]{1,0:T(8,128)(2,1)}), bf16[128,1088]{1,0:T(8,128)(2,1)}) %reduce-scatter.21.cloned.1.call-update) | async-done | bytes 278544
  415.8 50.5 %while.33 = (s32[]{:T(128)}, f32[1280,3,64]{0,2,1:T(8,128)}, f32[1280,3,64]{0,2,1:T(8,128)}, bf16[2,512,3,64]{1,3,2,0:T(8,128)(2,1)}, bf16[2,512,3,64]{1,3,2,0:T...) while((s32[]{:T(128)}, f32[1280,3,64]{0,2,1:T(8,128)}, ...), condition=%wide.region_14.15_spmd.clone.clone, body=%wide.region_12.14_spmd.clone.clone.sunk | while | flops 1279278848 | bytes 101538232 | solution.py:265
  419.7 6.4 multiply_reduce_fusion.3
  426.1 6.3 multiply_convert_fusion.5
  432.4 5.4 fusion.151
  444.8 6.3 multiply_reduce_fusion.3
  451.2 6.3 multiply_convert_fusion.5
  457.5 5.6 fusion.151
  478.6 35.2 %all_to_all.63 = bf16[1024,3,1,192]{3,1,2,0:T(4,128)(2,1)} all-to-all(bf16[1024,3,1,192]{3,1,2,0:T(4,128)(2,1)S(1)} %copy.100), channel_id=1, replica_groups=mesh['shard'=4,'heads'=4,'tensor'=2] {'heads','tensor'}, dimensions={0} | all-to-all | bytes 2359296 | tf_op jit(solution)/shard_map/all_to_all | solution.py:56
  518.1 7.4 fusion.73
  526.5 6.0 convolution_convert_fusion
  537.8 5.4 convolution_convert_fusion.3
  546.3 216.3 %reduce-scatter.13.cloned.1.call-done = f32[136,3264]{1,0:T(8,128)} async-done(((f32[1088,3264]{1,0:T(8,128)}), f32[136,3264]{1,0:T(8,128)}) %reduce-scatter.13.cloned.1.call-update) | async-done | bytes 1775632 | tf_op jit(solution)/shard_map/reduce_scatter | solution.py:303
  765.1 89.0 %reduce-scatter.17.cloned.1.call-done = bf16[544,1088]{1,0:T(8,128)(2,1)} async-done(((bf16[2176,1088]{1,0:T(8,128)(2,1)}), bf16[544,1088]{1,0:T(8,128)(2,1)}) %reduce-scatter.17.cloned.1.call-update) | async-done | bytes 1183760 | tf_op jit(solution)/shard_map/reduce_scatter | solution.py:220
  854.1 92.9 %reduce-scatter.15.cloned.1.call-done = bf16[1088,544]{0,1:T(8,128)(2,1)} async-done(((bf16[1088,2176]{0,1:T(8,128)(2,1)}), bf16[1088,544]{0,1:T(8,128)(2,1)}) %reduce-scatter.15.cloned.1.call-update) | async-done | bytes 1183760 | tf_op jit(solution)/shard_map/reduce_scatter | solution.py:217
  948.3 11.1 %all-reduce.17 = bf16[2176]{0:T(1024)(128)(2,1)S(1)} all-reduce(bf16[2176]{0:T(1024)(128)(2,1)S(1)} %copy-done.39), channel_id=15, replica_groups=mesh['shard'=4,'heads'=4,'tensor'=2] {'shard'}, use_global_device_ids=true, to_apply=%region_47.48.clone | all-reduce | flops 2176 | bytes 8704
  959.5 6.0 reduce-scatter.19.cloned.1.call-done
  974.5 36.7 %all-reduce.19 = (bf16[1088]{0:T(1024)(128)(2,1)S(1)}, bf16[1088]{0:T(1024)(128)(2,1)S(1)}, bf16[1088]{0:T(1024)(128)(2,1)S(1)}, bf16[1088]{0:T(1024)(128)(2,1)S...) all-reduce(f32[1088]{0:T(1024)S(1)} %get-tuple-element.367, ...), channel_id=8, replica_groups=mesh['shard'=4,'heads'=4,'tensor'=2] {'shard','tensor'}, use_global_device_ids=true, to_apply=%region_26.27.clone | all-reduce | flops 8704 | bytes 52224
  1011.9 5.7 all-reduce.21
  1022.7 24.8 %all-reduce.25.cloned.1.call-done = (bf16[136,3264]{1,0:T(8,128)(2,1)}, bf16[136,1088]{1,0:T(8,128)(2,1)}, bf16[1088,544]{0,1:T(8,128)(2,1)}, bf16[544,1088]{1,0:T(8,128)(2,1)}) async-done(((bf16[136,3264]{1,0:T(8,128)(2,1)}, bf16[136,1088]{1,0:T(8,128)(2,1)}, bf16[1088,544]{0,1:T(8,128)(2,1)}, bf16[544,1088]{1,0:T(8,128)(2,1)}), (bf16[136,3264]{1,0:T(8,128)(2,1)}, bf16[136,1088]{1,0:T(8,128)(2,1)}, ...) | async-done | bytes 3551248 | tf_op jit(solution)/shard_map/psum | solution.py:318
  (341 shorter events, 132.6 us)
Async XLA Ops:
  7.2 45.8 %copy-start.45 = (bf16[8,3]{1,0:T(8,128)(2,1)S(1)}, bf16[8,3]{1,0:T(8,128)(2,1)}, u32[]{:S(2)}) copy-start(bf16[8,3]{1,0:T(8,128)(2,1)} %constant.250) | copy-start | bytes 148
  7.2 46.1 %copy-start.53 = (s32[24]{0:T(128)S(1)}, s32[24]{0:T(128)}, u32[]{:S(2)}) copy-start(s32[24]{0:T(128)} %constant.254) | copy-start | bytes 292
  7.3 46.0 %copy-start.9 = (bf16[128,1088]{0,1:T(8,128)(2,1)S(1)}, bf16[128,1088]{0,1:T(8,128)(2,1)}, u32[]{:S(2)}) copy-start(bf16[128,1088]{0,1:T(8,128)(2,1)} %param.27) | copy-start | bytes 835588
  7.3 117.2 %all-gather.5.cloned.1.call-start = ((), (), s32[]{:S(2)}) async-start(), calls=%async_computation.10 | async-start | bytes 8146944 | tf_op jit(solution)/shard_map/all_gather | solution.py:115
  8.1 211.2 %all-gather.11.cloned.1.call-start = ((), (), s32[]{:S(2)}) async-start(), calls=%async_computation.13 | async-start | bytes 6266880 | tf_op jit(solution)/shard_map/all_gather | solution.py:196
  8.8 268.4 %all-gather.7.cloned.1.call-start = ((), (), s32[]{:S(2)}) async-start(), calls=%async_computation.11 | async-start | bytes 2820096 | tf_op jit(solution)/shard_map/all_gather | solution.py:116
  53.0 77.9 %copy-start.25 = (f32[1088]{0:T(1024)}, f32[1088]{0:T(1024)S(1)}, u32[]{:S(2)}) copy-start(f32[1088]{0:T(1024)S(1)} %convert_element_type.187) | copy-start | bytes 13060
  53.0 77.9 %copy-start.27 = (f32[1088]{0:T(1024)}, f32[1088]{0:T(1024)S(1)}, u32[]{:S(2)}) copy-start(f32[1088]{0:T(1024)S(1)} %convert_element_type.188) | copy-start | bytes 13060
  53.5 77.5 %copy-start.30 = (f32[128]{0:T(128)}, f32[128]{0:T(128)S(1)}, u32[]{:S(2)}) copy-start(f32[128]{0:T(128)S(1)} %broadcast_multiply_fusion.1) | copy-start | bytes 1540
  53.7 77.3 %copy-start.50 = (f32[128]{0:T(128)}, f32[128]{0:T(128)S(1)}, u32[]{:S(2)}) copy-start(f32[128]{0:T(128)S(1)} %fusion.62) | copy-start | bytes 1540
  53.7 77.3 %copy-start.34 = (f32[128]{0:T(128)}, f32[128]{0:T(128)S(1)}, u32[]{:S(2)}) copy-start(f32[128]{0:T(128)S(1)} %fusion.71) | copy-start | bytes 1540
  133.2 17.0 %copy-start.52 = (s32[17]{0:T(128)S(1)}, s32[17]{0:T(128)}, u32[]{:S(2)}) copy-start(s32[17]{0:T(128)} %constant.255) | copy-start | bytes 208
  133.2 19.6 %all-to-all-start = ((bf16[128,3,8,192]{0,3,1,2:T(8,128)(2,1)}), bf16[128,3,8,192]{0,3,1,2:T(8,128)(2,1)S(1)}, u32[]{:S(2)}, u32[]{:S(2)}) async-start(bf16[128,3,8,192]{0,3,1,2:T(8,128)(2,1)} %copy.88), calls=%async_computation | async-start | bytes 2359296 | tf_op jit(solution)/shard_map/all_to_all | solution.py:52
  136.9 234.6 %all-gather.9.cloned.1.call-start = ((), (), s32[]{:S(2)}) async-start(), calls=%async_computation.12 | async-start | bytes 6266880 | tf_op jit(solution)/shard_map/all_gather | solution.py:195
  150.3 76.2 %copy-start.38 = (s32[1024]{0:T(1024)}, s32[1024]{0:T(1024)S(1)}, u32[]{:S(2)}) copy-start(s32[1024]{0:T(1024)S(1)} %pad_clamp_fusion) | copy-start | bytes 12292
  153.0 10.8 %collective-permute-start = (bf16[256,2,192]{0,2,1:T(8,128)(2,1)S(1)}, bf16[256,2,192]{0,2,1:T(8,128)(2,1)S(1)}, u32[]{:S(2)}, u32[]{:S(2)}) collective-permute-start(bf16[256,2,192]{0,2,1:T(8,128)(2,1)S(1)} %slice_bitcast_fusion.2), channel_id=1, source_target_pairs={{0,8},{8,16},{16,24},{1,9},{9,17},{17,25},{2,10},{10,18},{18,26},{... | collective-permute-start | bytes 589832 | tf_op jit(solution)/shard_map/ppermute | solution.py:19
  182.1 42.9 %all-to-all-start.1 = ((bf16[8,2,12288]{2,1,0:T(2,128)(2,1)}), bf16[8,2,12288]{2,1,0:T(2,128)(2,1)S(1)}, u32[]{:S(2)}, u32[]{:S(2)}) async-start(bf16[8,2,12288]{2,1,0:T(2,128)(2,1)} %reshape.616), calls=%async_computation.1 | async-start | bytes 786432 | tf_op jit(solution)/shard_map/all_to_all | solution.py:56
  185.5 211.6 %reduce-scatter.21.cloned.1.call-start = ((), (), s32[]{:S(2)}) async-start(), calls=%async_computation.18 | async-start | bytes 884736
  280.1 119.7 %copy-start.7 = (f32[128,1088]{0,1:T(8,128)}, f32[128,1088]{0,1:T(8,128)S(1)}, u32[]{:S(2)}) copy-start(f32[128,1088]{0,1:T(8,128)S(1)} %get-tuple-element.469) | copy-start | bytes 1671172
  280.1 119.7 %copy-start.32 = (f32[128]{0:T(128)}, f32[128]{0:T(128)S(1)}, u32[]{:S(2)}) copy-start(f32[128]{0:T(128)S(1)} %broadcast_multiply_fusion) | copy-start | bytes 1540
  280.3 119.5 %copy-start.36 = (f32[128]{0:T(128)}, f32[128]{0:T(128)S(1)}, u32[]{:S(2)}) copy-start(f32[128]{0:T(128)S(1)} %fusion.72) | copy-start | bytes 1540
  288.7 90.4 %copy-start.13 = (bf16[256,1088]{0,1:T(8,128)(2,1)}, bf16[256,1088]{0,1:T(8,128)(2,1)S(1)}, u32[]{:S(2)}) copy-start(bf16[256,1088]{0,1:T(8,128)(2,1)S(1)} %all_gather.51) | copy-start | bytes 1671172
  403.7 10.8 %all-to-all-start.2 = ((bf16[128,1,8,192]{0,3,1,2:T(8,128)(2,1)}), bf16[128,1,8,192]{0,3,1,2:T(8,128)(2,1)S(1)}, u32[]{:S(2)}, u32[]{:S(2)}) async-start(bf16[128,1,8,192]{0,3,1,2:T(8,128)(2,1)} %multiply_bitcast_fusion), calls=%async_computation.2 | async-start | bytes 786432 | tf_op jit(solution)/shard_map/all_to_all | solution.py:52
  407.2 137.3 %reduce-scatter.23.cloned.1.call-start = ((), (), s32[]{:S(2)}) async-start(), calls=%async_computation.19 | async-start | bytes 5640192
  410.4 352.2 %reduce-scatter.13.cloned.1.call-start = ((), (), s32[]{:S(2)}) async-start(), calls=%async_computation.14 | async-start | bytes 16293888 | tf_op jit(solution)/shard_map/reduce_scatter | solution.py:303
  468.2 8.7 collective-permute-start.1
  525.5 328.6 %reduce-scatter.17.cloned.1.call-start = ((), (), s32[]{:S(2)}) async-start(), calls=%async_computation.16 | async-start | bytes 6266880 | tf_op jit(solution)/shard_map/reduce_scatter | solution.py:220
  532.5 414.5 %reduce-scatter.15.cloned.1.call-start = ((), (), s32[]{:S(2)}) async-start(), calls=%async_computation.15 | async-start | bytes 6266880 | tf_op jit(solution)/shard_map/reduce_scatter | solution.py:217
  537.8 427.7 %reduce-scatter.19.cloned.1.call-start = ((), (), s32[]{:S(2)}) async-start(), calls=%async_computation.17 | async-start | bytes 884736
  544.4 503.2 %all-reduce.25.cloned.1.call-start = ((), (), s32[]{:S(2)}) async-start(), calls=%async_computation.20 | async-start | bytes 7450624 | tf_op jit(solution)/shard_map/psum | solution.py:318
  765.1 181.9 %copy-start.42 = (bf16[1088]{0:T(1024)(128)(2,1)S(1)}, bf16[1088]{0:T(1024)(128)(2,1)}, u32[]{:S(2)}) copy-start(bf16[1088]{0:T(1024)(128)(2,1)} %get-tuple-element.426) | copy-start | bytes 6532
  765.1 183.2 %copy-start.39 = (bf16[2176]{0:T(1024)(128)(2,1)S(1)}, bf16[2176]{0:T(1024)(128)(2,1)}, u32[]{:S(2)}) copy-start(bf16[2176]{0:T(1024)(128)(2,1)} %get-tuple-element.440) | copy-start | bytes 13060
  (56 other events, 200.2 us)
Sparse Core Ops, SparseCore 0:
  10.3 114.1 all-gather.4
  126.1 93.1 all-gather.10
  221.5 55.7 all-gather.6
  278.6 92.8 all-gather.8
  383.4 13.6 reduce-scatter.20
  411.8 115.0 reduce-scatter.22
  530.6 231.9 reduce-scatter.12
  764.9 89.1 reduce-scatter.16
  856.4 90.5 reduce-scatter.14
  949.7 15.7 reduce-scatter.18
  968.9 78.6 all-reduce.24
where the time goes:
time: 1070 us; the launch traced here: 1060 us
  waiting for transfers between devices  699 us (65%)
  blocking collectives  147 us (14%)
  matrix products  97.9 us (9%)
  other arithmetic  45.9 us (4%)
  local copies, waits for them, and re-layouts  37.7 us (4%)
  between operations  18.7 us (2%)
  starting transfers between devices  14.9 us (1%)
    reduce_scatter x1, waiting for transfers between devices, shards(): lax.psum_scatter(g_attend, ('shard', 'tensor'), scatter_dimension=0, tile...  216 us
    unnamed x4, blocking collectives  98.4 us
    reduce_scatter x1, waiting for transfers between devices, shards(): lax.psum_scatter(g_up.astype(jnp.bfloat16), 'shard', scatter_dimension=1,...  92.9 us
    reduce_scatter x1, waiting for transfers between devices, shards(): lax.psum_scatter(g_down.astype(jnp.bfloat16), 'shard', scatter_dimension=...  89 us
    all_gather x1, waiting for transfers between devices, shards(): lax.all_gather(up_weight, 'shard', axis=1, tiled=True)  82.8 us
    all_gather x1, waiting for transfers between devices, shards(): lax.all_gather(attend_weight, ('shard', 'tensor'), axis=0, tiled=True)  70.8 us
    all_gather x1, waiting for transfers between devices, shards(): lax.all_gather(out_weight, ('shard', 'tensor'), axis=0, tiled=True)  50.1 us
    all_to_all x1, blocking collectives, to_tokens(): lax.all_to_all(values, ('heads', 'tensor'), split_axis=0, concat_axis=2,...  35.2 us
  transfers between devices with their start and end apart: 16, of which 14 were waited for; matrix products, arithmetic and copies ran while one was open for 14% of the time, Pallas kernels for 0%

commit v1 on v0

v1 whole, which is shorter than its diff:
```python
import jax
import jax.numpy as jnp
from jax import lax
from jax.sharding import PartitionSpec as P

NH = 17
HD = 64
SLOTS = 3


EPS = 1e-05
NEG = -1e30


def from_behind(value, axis, steps):
    count = lax.axis_size(axis)
    leading, last = (max(0, -steps), min(count, count - steps))
    return lax.ppermute(value, axis, [(source, source + steps) for source in range(leading, last)])


def layer_norm(values, gain_vec, shift_vec):
    center = values - jnp.mean(values, axis=-1, keepdims=True)
    spread = jnp.mean(center * center, axis=-1, keepdims=True)
    return center * lax.rsqrt(spread + EPS) * gain_vec + shift_vec


def gelu_tanh(values):
    return jax.nn.gelu(values, approximate=True)


def block_scores(query_part, key_rows, bounds, first_query, prev_tok):
    scores = jnp.einsum("qhd,khd->hqk", query_part, key_rows, preferred_element_type=jnp.float32)
    local_query = first_query + jnp.arange(query_part.shape[0], dtype=jnp.int32)
    local_key = jnp.arange(key_rows.shape[0], dtype=jnp.int32) - prev_tok
    start = jnp.where(local_query >= bounds[0], bounds[0], bounds[1])
    allowed = (local_key[None, :] >= start[:, None]) & (local_key[None, :] <= local_query[:, None])
    return jnp.where(allowed[None], scores * HD ** (-0.5), NEG)


def attend(query_flat, key_flat, value_flat, bounds, prev_tok):
    group_tok = query_flat.shape[0]
    block = group_tok // 2
    results, totals = [], []
    for first in range(0, group_tok, block):
        last_key = first + block + prev_tok
        query_part = query_flat[first : first + block].reshape(block, SLOTS, HD)
        key_rows = key_flat[:last_key].reshape(last_key, SLOTS, HD)
        value_rows = value_flat[:last_key].reshape(last_key, SLOTS, HD)
        scores = block_scores(query_part, key_rows, bounds, first, prev_tok)
        row_max = jnp.max(scores, axis=-1, keepdims=True)
        exp_scores = jnp.exp(scores - row_max)
        row_total = jnp.sum(exp_scores, axis=-1, keepdims=True)
        weights = (exp_scores / row_total).astype(jnp.bfloat16)
        result = jnp.einsum("hqk,khd->qhd", weights, value_rows, preferred_element_type=jnp.float32)
        results.append(result.astype(jnp.bfloat16).reshape(block, SLOTS * HD))
        totals.append((row_max + jnp.log(row_total))[..., 0])
    return jnp.concatenate(results, axis=0), totals


def attend_back(query_flat, key_flat, value_flat, d_flat, totals, bounds, prev_tok):
    group_tok = query_flat.shape[0]
    block = group_tok // 2
    key_grad, value_grad, query_grads = 0.0, 0.0, []
    for step, first in enumerate(range(0, group_tok, block)):
        last_key = first + block + prev_tok
        rest = key_flat.shape[0] - last_key
        query_part = query_flat[first : first + block].reshape(block, SLOTS, HD)
        d_part = d_flat[first : first + block].reshape(block, SLOTS, HD)
        key_rows = key_flat[:last_key].reshape(last_key, SLOTS, HD)
        value_rows = value_flat[:last_key].reshape(last_key, SLOTS, HD)
        scores = block_scores(query_part, key_rows, bounds, first, prev_tok)
        probs = jnp.exp(scores - totals[step][..., None])
        d_probs = jnp.einsum("qhd,khd->hqk", d_part, value_rows, preferred_element_type=jnp.float32)
        row_inner = jnp.sum(probs * d_probs, axis=-1, keepdims=True)
        d_scores = (probs * (d_probs - row_inner)).astype(jnp.bfloat16)
        query_grads.append(
            jnp.einsum("hqk,khd->qhd", d_scores, key_rows, preferred_element_type=jnp.float32)
            .reshape(block, SLOTS * HD)
            * HD ** (-0.5)
        )
        part = jnp.einsum("hqk,qhd->khd", d_scores, query_part, preferred_element_type=jnp.float32)
        key_grad += jnp.pad(part.reshape(last_key, SLOTS * HD) * HD ** (-0.5), ((0, rest), (0, 0)))
        part = jnp.einsum(
            "hqk,qhd->khd", probs.astype(jnp.bfloat16), d_part, preferred_element_type=jnp.float32
        )
        value_grad += jnp.pad(part.reshape(last_key, SLOTS * HD), ((0, rest), (0, 0)))
    return jnp.concatenate(query_grads, axis=0), key_grad, value_grad


TEAM = ("heads", "tensor")
OWNERS = ("shard", "tensor")


def set_bounds(group_total, tensor_total):
    base_count, extra_count = NH // group_total, NH % group_total
    firsts, counts = [], []
    next_head = 0
    for group_idx in range(group_total):
        group_size = base_count + (1 if group_idx < extra_count else 0)
        larger = -(-group_size // tensor_total)
        for tensor_pos in range(tensor_total):
            filled = max(0, min(larger, group_size - tensor_pos * larger))
            firsts.append(next_head)
            counts.append(filled)
            next_head += filled
    return firsts, counts


def team_sum(values):
    return lax.psum_scatter(
        values.astype(jnp.bfloat16), TEAM, scatter_dimension=0, tiled=True
    ).astype(jnp.float32)


def swap_team(values):
    return lax.all_to_all(values, TEAM, split_axis=0, concat_axis=0, tiled=True)


def dot_nt(left, right):
    return lax.dot_general(
        left, right, (((1,), (1,)), ((), ())), preferred_element_type=jnp.float32
    )


def dot_tn(left, right):
    return lax.dot_general(
        left, right, (((0,), (0,)), ((), ())), preferred_element_type=jnp.float32
    )


def shards(
    tokens,
    cotangent,
    cut_pos,
    attend_weight,
    out_weight,
    up_weight,
    down_weight,
    first_gain,
    first_bias,
    query_bias,
    value_bias,
    out_bias,
    second_gain,
    second_bias,
    up_bias,
    down_bias,
):
    tok_rows, width = tokens.shape
    heads_count = lax.axis_size("heads")
    tensor_count = lax.axis_size("tensor")
    shard_count = lax.axis_size("shard")
    team = heads_count * tensor_count
    group_tok = tok_rows * team
    prev_tok = group_tok // 4
    key_count = group_tok + prev_tok
    score_scale = HD ** (-0.5)
    slot_width = SLOTS * HD
    shard_idx = lax.axis_index("shard")
    heads_idx = lax.axis_index("heads")
    tensor_idx = lax.axis_index("tensor")
    set_idx = heads_idx * tensor_count + tensor_idx
    firsts, counts = set_bounds(heads_count, tensor_count)
    first_table = jnp.array(firsts, jnp.int32)
    count_table = jnp.array(counts, jnp.int32)
    my_first = first_table[set_idx]
    my_count = count_table[set_idx]
    slot_valid = jnp.arange(SLOTS) < my_count
    group_first = first_table[heads_idx * tensor_count]
    group_heads = max(
        sum(counts[g * tensor_count : (g + 1) * tensor_count]) for g in range(heads_count)
    )
    group_span = max(
        firsts[j] - firsts[j // tensor_count * tensor_count] + SLOTS for j in range(team)
    )
    group_span = max(group_span, group_heads)
    padded_heads = max(max(firsts) + SLOTS, max(firsts[::tensor_count]) + group_span, NH)
    own_rows = attend_weight.shape[0]
    hidden_own = up_weight.shape[1]
    hidden_part = hidden_own // heads_count

    cut_columns = 3 * group_span * HD
    per_head = jnp.pad(
        attend_weight.reshape(own_rows, 3, NH, HD),
        ((0, 0), (0, 0), (0, padded_heads - NH), (0, 0)),
    )
    group_part = lax.dynamic_slice_in_dim(per_head, group_first, group_span, 2)
    vectors = jnp.concatenate(
        [
            first_gain,
            first_bias,
            query_bias,
            value_bias,
            out_bias,
            second_gain,
            second_bias,
            down_bias,
            up_bias,
        ]
    )
    vector_rows = -(-vectors.shape[0] // cut_columns)
    vectors = jnp.pad(vectors, (0, vector_rows * cut_columns - vectors.shape[0]))
    packed = jnp.concatenate(
        [group_part.reshape(own_rows, cut_columns), vectors.reshape(vector_rows, cut_columns)],
        axis=0,
    )
    token_all = lax.all_gather(tokens, TEAM, axis=0, tiled=True)
    packed_all = lax.all_gather(packed, OWNERS, axis=0, tiled=False)
    vector_all = packed_all[:, own_rows:].reshape(shard_count * tensor_count, -1)
    (
        gain_one,
        shift_one,
        bias_query,
        bias_value,
        bias_out,
        gain_two,
        shift_two,
        bias_down,
    ) = (
        vector_all[:, member * own_rows : (member + 1) * own_rows]
        .reshape(width)
        .astype(jnp.float32)
        for member in range(8)
    )
    bias_up = vector_all[:, 8 * own_rows : 8 * own_rows + hidden_own].reshape(
        shard_count, tensor_count, heads_count, hidden_part
    )
    bias_up = lax.dynamic_slice(
        bias_up, (0, tensor_idx, heads_idx, 0), (shard_count, 1, 1, hidden_part)
    ).reshape(shard_count * hidden_part)
    w_set = lax.dynamic_slice_in_dim(
        packed_all[:, :own_rows].reshape(width, 3, group_span, HD), my_first - group_first, SLOTS, 2
    )
    w_set = jnp.where(slot_valid[None, None, :, None], w_set, 0).reshape(width, 3 * slot_width)

    def set_vector(vector):
        slots = jnp.pad(vector.reshape(NH, HD), ((0, padded_heads - NH), (0, 0)))
        slots = lax.dynamic_slice_in_dim(slots, my_first, SLOTS, 0)
        return jnp.where(slot_valid[:, None], slots, 0).reshape(slot_width)

    bias_set = jnp.concatenate(
        [set_vector(bias_query), jnp.zeros((slot_width,), jnp.float32), set_vector(bias_value)]
    )
    w_out = lax.all_gather(out_weight, OWNERS, axis=0, tiled=False).reshape(width, width)
    feed_part = jnp.concatenate(
        [
            lax.dynamic_slice_in_dim(up_weight, heads_idx * hidden_part, hidden_part, 1).T,
            lax.dynamic_slice_in_dim(down_weight, heads_idx * hidden_part, hidden_part, 0),
        ],
        axis=1,
    )
    feed_all = lax.all_gather(feed_part, "shard", axis=0, tiled=False).reshape(
        shard_count * hidden_part, 2 * width
    )
    w_up, w_down = feed_all[:, :width], feed_all[:, width:]
    grad_all = lax.all_gather(cotangent, "heads", axis=0, tiled=True)

    token_f = token_all.astype(jnp.float32)
    center = token_f - jnp.mean(token_f, axis=-1, keepdims=True)
    inverse = lax.rsqrt(jnp.mean(center * center, axis=-1, keepdims=True) + EPS)
    unit = center * inverse
    normed = (unit * gain_one + shift_one).astype(jnp.bfloat16)
    projected = (
        jnp.dot(normed, w_set, preferred_element_type=jnp.float32) + bias_set
    ).astype(jnp.bfloat16)
    query_flat = projected[:, :slot_width]
    own_pair = projected[:, slot_width:]
    earlier = from_behind(own_pair[group_tok - prev_tok :], "shard", 1)
    pair_rows = jnp.concatenate([earlier, own_pair], axis=0)
    key_flat, value_flat = pair_rows[:, :slot_width], pair_rows[:, slot_width:]
    cut_here = cut_pos[shard_idx]
    cut_before = cut_pos[jnp.maximum(shard_idx - 1, 0)]
    earlier_start = jnp.where(shard_idx > 0, cut_before - group_tok, 0)
    bounds = jnp.stack([cut_here, earlier_start]).astype(jnp.int32)
    attended, log_totals = attend(query_flat, key_flat, value_flat, bounds, prev_tok)
    returned = swap_team(attended.reshape(team, tok_rows, slot_width))
    attn_tok = jnp.concatenate(
        [returned[member, :, : counts[member] * HD] for member in range(team)], axis=1
    )
    own_tok_f = tokens.astype(jnp.float32)
    branch_f = jnp.dot(attn_tok, w_out, preferred_element_type=jnp.float32)
    resid = own_tok_f + branch_f + bias_out
    normed_two_f, norm_two_back = jax.vjp(layer_norm, resid, gain_two, shift_two)
    normed_two = normed_two_f.astype(jnp.bfloat16)

    own_grad_rows = lax.dynamic_slice_in_dim(cotangent, tensor_idx * tok_rows, tok_rows, 0)
    d_act = dot_nt(grad_all, w_down)
    feed_rows = lax.all_gather(normed_two, TEAM, axis=0, tiled=True)
    hidden_pre = dot_nt(feed_rows, w_up) + bias_up.astype(jnp.float32)
    hidden_act_f, gelu_back = jax.vjp(gelu_tanh, hidden_pre)
    hidden_act = hidden_act_f.astype(jnp.bfloat16)
    (d_pre_f,) = gelu_back(d_act)
    d_pre = d_pre_f.astype(jnp.bfloat16)
    d_normed_two = team_sum(jnp.dot(d_pre, w_up, preferred_element_type=jnp.float32))
    partial_out = jnp.dot(hidden_act, w_down, preferred_element_type=jnp.float32)
    fed_rows = team_sum(partial_out)
    layer_out = (resid + fed_rows + bias_down).astype(jnp.bfloat16)
    g_feed = jnp.concatenate([dot_tn(d_pre, feed_rows), dot_tn(hidden_act, grad_all)], axis=1)
    g_bias_up = jnp.sum(d_pre.astype(jnp.float32), axis=0)
    g_feed = lax.psum_scatter(
        g_feed.astype(jnp.bfloat16).reshape(shard_count, hidden_part, 2 * width),
        "shard",
        scatter_dimension=0,
        tiled=False,
    )
    g_feed = lax.all_gather(g_feed, "heads", axis=0, tiled=False).reshape(hidden_own, 2 * width)
    g_up = g_feed[:, :width].T.astype(jnp.float32)
    g_down = g_feed[:, width:].astype(jnp.float32)

    own_grad_f = own_grad_rows.astype(jnp.float32)
    g_bias_down = jnp.sum(own_grad_f, axis=0)
    d_resid_norm, g_gain_two, g_shift_two = norm_two_back(d_normed_two)
    d_resid = own_grad_f + d_resid_norm
    d_branch = d_resid.astype(jnp.bfloat16)
    g_bias_out = jnp.sum(d_branch.astype(jnp.float32), axis=0)
    d_attended = dot_nt(d_branch, w_out).astype(jnp.bfloat16)
    d_sets = jnp.stack(
        [
            jnp.pad(
                d_attended[:, firsts[member] * HD : (firsts[member] + counts[member]) * HD],
                ((0, 0), (0, slot_width - counts[member] * HD)),
            )
            for member in range(team)
        ],
        axis=0,
    )
    d_flat = swap_team(d_sets).reshape(group_tok, slot_width)
    g_out = dot_tn(attn_tok, d_branch)
    g_out = lax.psum_scatter(
        g_out.astype(jnp.bfloat16).reshape(shard_count * tensor_count, own_rows, width),
        OWNERS,
        scatter_dimension=0,
        tiled=False,
    )
    g_out = lax.psum(g_out, "heads").astype(jnp.float32)

    query_grad, key_grad, value_grad = attend_back(
        query_flat, key_flat, value_flat, d_flat, log_totals, bounds, prev_tok
    )
    spill = jnp.concatenate([key_grad[:prev_tok], value_grad[:prev_tok]], axis=1)
    later = from_behind(spill.astype(jnp.bfloat16), "shard", -1).astype(jnp.float32)
    later = jnp.pad(later, ((group_tok - prev_tok, 0), (0, 0)))
    own_grads = jnp.concatenate([key_grad[prev_tok:], value_grad[prev_tok:]], axis=1) + later
    d_projected = jnp.concatenate(
        [query_grad.astype(jnp.bfloat16), own_grads.astype(jnp.bfloat16)], axis=1
    )
    d_normed_part = dot_nt(d_projected, w_set)
    d_normed = team_sum(d_normed_part)
    g_attend = dot_tn(normed, d_projected)
    g_attend = lax.psum_scatter(
        g_attend.astype(jnp.bfloat16).reshape(
            shard_count, tensor_count * own_rows, 3 * slot_width
        ),
        "shard",
        scatter_dimension=0,
        tiled=False,
    )
    g_attend = lax.all_to_all(
        g_attend.reshape(tensor_count, own_rows, 3 * slot_width),
        "tensor",
        split_axis=0,
        concat_axis=0,
        tiled=True,
    )
    g_attend = lax.all_gather(g_attend, "heads", axis=0, tiled=False).reshape(
        team, own_rows, 3, slot_width
    )
    g_attend = jnp.concatenate(
        [
            g_attend[member, :, part, : counts[member] * HD]
            for part in range(3)
            for member in range(team)
        ],
        axis=1,
    ).astype(jnp.float32)

    d_sum = jnp.sum(d_projected.astype(jnp.float32), axis=0)

    def place_vector(vector):
        spread = jnp.zeros((padded_heads, HD), jnp.float32)
        slots = jnp.where(slot_valid[:, None], vector.reshape(SLOTS, HD), 0)
        return lax.dynamic_update_slice_in_dim(spread, slots, my_first, 0)[:NH].reshape(width)

    g_bias_up_all = lax.dynamic_update_slice(
        jnp.zeros((shard_count, tensor_count, heads_count, hidden_part), jnp.float32),
        g_bias_up.reshape(shard_count, 1, 1, hidden_part),
        (0, tensor_idx, heads_idx, 0),
    ).reshape(-1)
    terms = jnp.concatenate(
        [
            jnp.sum(d_normed_part * unit, axis=0),
            jnp.sum(d_normed_part, axis=0),
            place_vector(d_sum[:slot_width]),
            place_vector(d_sum[2 * slot_width :]),
            g_bias_out,
            g_gain_two,
            g_shift_two,
            g_bias_down,
            g_bias_up_all,
        ]
    )
    sums = lax.psum(terms, ("shard", "heads", "tensor"))
    owner = shard_idx * tensor_count + tensor_idx
    (
        s_gain_one,
        s_shift_one,
        s_bias_query,
        s_bias_value,
        s_bias_out,
        s_gain_two,
        s_shift_two,
        s_bias_down,
    ) = (
        lax.dynamic_slice_in_dim(sums, member * width + owner * own_rows, own_rows, 0)
        for member in range(8)
    )
    s_bias_up = lax.dynamic_slice_in_dim(sums, 8 * width + owner * hidden_own, hidden_own, 0)

    own_center = own_tok_f - jnp.mean(own_tok_f, axis=-1, keepdims=True)
    own_inverse = lax.rsqrt(jnp.mean(own_center * own_center, axis=-1, keepdims=True) + EPS)
    own_unit = own_center * own_inverse
    scaled = d_normed * gain_one
    tokens_grad = d_resid + own_inverse * (
        scaled
        - jnp.mean(scaled, axis=-1, keepdims=True)
        - own_unit * jnp.mean(scaled * own_unit, axis=-1, keepdims=True)
    )
    return (
        layer_out,
        tokens_grad,
        g_attend,
        g_out,
        g_up,
        g_down,
        s_gain_one,
        s_shift_one,
        s_bias_query,
        s_bias_value,
        s_bias_out,
        s_gain_two,
        s_shift_two,
        s_bias_up,
        s_bias_down,
    )


def solution(mesh):
    placed = (
        P(("shard", "heads", "tensor"), None),
        P(("shard", "heads"), None),
        P(),
        P(("shard", "tensor"), None),
        P(("shard", "tensor"), None),
        P(None, ("shard", "tensor")),
        P(("shard", "tensor"), None),
        P(("shard", "tensor")),
        P(("shard", "tensor")),
        P(("shard", "tensor")),
        P(("shard", "tensor")),
        P(("shard", "tensor")),
        P(("shard", "tensor")),
        P(("shard", "tensor")),
        P(("shard", "tensor")),
        P(("shard", "tensor")),
    )
    return jax.shard_map(
        shards,
        mesh=mesh,
        in_specs=placed,
        out_specs=(
            P(("shard", "heads", "tensor"), None),
            P(("shard", "heads", "tensor"), None),
            P(("shard", "tensor"), None),
            P(("shard", "tensor"), None),
            P(None, ("shard", "tensor")),
            P(("shard", "tensor"), None),
            P(("shard", "tensor")),
            P(("shard", "tensor")),
            P(("shard", "tensor")),
            P(("shard", "tensor")),
            P(("shard", "tensor")),
            P(("shard", "tensor")),
            P(("shard", "tensor")),
            P(("shard", "tensor")),
            P(("shard", "tensor")),
        ),
        check_vma=False,
    )
```

time: 1070 us -> 681 us (0.64)
  waiting for transfers between devices: 699 us -> 409 us
  blocking collectives: 147 us -> 39.9 us
  local copies, waits for them, and re-layouts: 37.7 us -> 85.3 us
  matrix products: 97.9 us -> 65.9 us
  other arithmetic: 45.9 us -> 33.3 us
    reduce_scatter x3 -> x1, waiting for transfers between devices: 398 us -> 34.2 us  [shards(): lax.psum_scatter(g_attend.astype(jnp.bfloat16).reshape(shard_count, tenso...]
    unnamed x14 -> x20, waiting for transfers between devices: 22.5 us -> 159 us
    unnamed x4 -> x0, blocking collectives: 98.4 us -> none
    all_gather x4 -> x8, waiting for transfers between devices: 237 us -> 183 us  [the longest x1 54.8 us: shards(): packed_all = lax.all_gather(packed, OWNERS, axis=0, tiled=False)]
    all_to_all x1 -> x0, blocking collectives: 35.2 us -> none  [to_tokens(): lax.all_to_all(values, ('heads', 'tensor'), split_axis=0, concat_axis=2,...]
    psum x1, blocking collectives: 5.74 us -> 39.9 us  [shards(): sums = lax.psum(terms, ('shard', 'heads', 'tensor'))]
    psum x1, waiting for transfers between devices: 24.8 us -> 0.01 us  [shards(): g_out = lax.psum(g_out, 'heads').astype(jnp.float32)]
    unnamed x146 -> x174, local copies, waits for them, and re-layouts: 14.6 us -> 33.9 us
  transfers between devices with their start and end apart: 16 -> 20, of which waited for: 14 -> 16; matrix products, arithmetic and copies ran while one was open for 14% -> 22% of each run, Pallas kernels for 0% -> 0%
where the time goes in v1:
time: 681 us; the launch traced here: 673 us
  waiting for transfers between devices  409 us (60%)
  local copies, waits for them, and re-layouts  85.3 us (13%)
  matrix products  65.9 us (10%)
  blocking collectives  39.9 us (6%)
  other arithmetic  33.3 us (5%)
  between operations  21.7 us (3%)
  starting transfers between devices  18.1 us (3%)
    unnamed x20, waiting for transfers between devices  159 us
    all_gather x1, waiting for transfers between devices, shards(): packed_all = lax.all_gather(packed, OWNERS, axis=0, tiled=False)  54.8 us
    psum x1, blocking collectives, shards(): sums = lax.psum(terms, ('shard', 'heads', 'tensor'))  39.9 us
    all_gather x1, waiting for transfers between devices, shards(): lax.all_gather(feed_part, 'shard', axis=0, tiled=False)  39.4 us
    reduce_scatter x1, waiting for transfers between devices, shards(): lax.psum_scatter(g_attend.astype(jnp.bfloat16).reshape(shard_count, tenso...  34.2 us
    unnamed x174, local copies, waits for them, and re-layouts  33.9 us
    all_gather x1, waiting for transfers between devices, shards(): feed_rows = lax.all_gather(normed_two, TEAM, axis=0, tiled=True)  29.9 us
    all_gather x1, waiting for transfers between devices, shards(): grad_all = lax.all_gather(cotangent, 'heads', axis=0, tiled=True)  20.1 us
  transfers between devices with their start and end apart: 20, of which 16 were waited for; matrix products, arithmetic and copies ran while one was open for 22% of the time, Pallas kernels for 0%

profile of v1, /device:TPU:0, one launch (start us, length us, event | category | flops | bytes accessed | tf_op | source)
XLA Modules:
  0.0 673.3 jit_solution(14439077298568559730)
XLA Ops:
  10.6 6.1 concatenate.50
  32.7 8.7 %all-gather.14.cloned.1.call-done = bf16[1024,1088]{0,1:T(8,128)(2,1)} async-done(((bf16[128,1088]{0,1:T(8,128)(2,1)}), bf16[1024,1088]{0,1:T(8,128)(2,1)}) %all-gather.14.cloned.1.call-update) | async-done | bytes 2228240 | tf_op jit(solution)/shard_map/all_gather | solution.py:207
  44.4 54.8 %all-gather.28.cloned.1.call-done = bf16[8,138,1152]{2,1,0:T(8,128)(2,1)} async-done(((bf16[1,138,1152]{2,1,0:T(8,128)(2,1)}), bf16[8,138,1152]{2,1,0:T(8,128)(2,1)}) %all-gather.28.cloned.1.call-update) | async-done | bytes 2543632 | tf_op jit(solution)/shard_map/all_gather | solution.py:208
  104.8 7.2 %copy.142 = bf16[8,136,1152]{1,0,2:T(8,128)(2,1)} copy(bf16[8,136,1152]{2,1,0:T(8,128)(2,1)} %slice.322) | data formatting | bytes 5013504 | tf_op jit(solution)/shard_map/slice | solution.py:232
  112.0 8.1 %reshape.467 = bf16[1088,3,6,64]{0,3,2,1:T(8,128)(2,1)} reshape(bf16[8,136,1152]{1,0,2:T(8,128)(2,1)} %copy.142) | data formatting | bytes 5013504 | tf_op jit(solution)/shard_map/reshape | solution.py:232
  124.8 3.9 collective-permute-start
  128.7 8.0 %collective-permute-done = bf16[256,384]{0,1:T(8,128)(2,1)S(1)} collective-permute-done((bf16[256,384]{0,1:T(8,128)(2,1)S(1)}, bf16[256,384]{0,1:T(8,128)(2,1)S(1)}, u32[]{:S(2)}, u32[]{:S(2)}) %collective-permute-start) | collective-permute-done | bytes 196640 | tf_op jit(solution)/shard_map/ppermute | solution.py:18
  153.1 7.0 %all-to-all-done = bf16[8,128,192]{1,2,0:T(8,128)(2,1)S(1)} async-done(((bf16[8,128,192]{1,2,0:T(8,128)(2,1)}), bf16[8,128,192]{1,2,0:T(8,128)(2,1)S(1)}, u32[]{:S(2)}, u32[]{:S(2)}) %all-to-all-start) | async-done | bytes 393248 | tf_op jit(solution)/shard_map/all_to_all | solution.py:116
  166.1 39.4 %all-gather.24.cloned.1.call-done = bf16[544,2176]{1,0:T(8,128)(2,1)} async-done(((bf16[136,2176]{1,0:T(8,128)(2,1)}), bf16[544,2176]{1,0:T(8,128)(2,1)}) %all-gather.24.cloned.1.call-update) | async-done | bytes 2367504 | tf_op jit(solution)/shard_map/all_gather | solution.py:252
  205.5 29.9 %all-gather.16.cloned.1.call-done = bf16[1024,1088]{0,1:T(8,128)(2,1)} async-done(((bf16[128,1088]{0,1:T(8,128)(2,1)}), bf16[1024,1088]{0,1:T(8,128)(2,1)}) %all-gather.16.cloned.1.call-update) | async-done | bytes 2228240 | tf_op jit(solution)/shard_map/all_gather | solution.py:288
  235.5 5.0 fusion.40
  240.4 20.1 %all-gather.18.cloned.1.call-done = bf16[1024,1088]{0,1:T(8,128)(2,1)} async-done(((bf16[256,1088]{0,1:T(8,128)(2,1)}), bf16[1024,1088]{0,1:T(8,128)(2,1)}) %all-gather.18.cloned.1.call-update) | async-done | bytes 2228240 | tf_op jit(solution)/shard_map/all_gather | solution.py:256
  260.5 5.7 convert_reduce_fusion.2
  270.6 4.1 copy.163
  274.8 42.6 %reduce-scatter.21.cloned.1.call-done = bf16[128,1088]{1,0:T(8,128)(2,1)} async-done(((bf16[1024,1088]{1,0:T(8,128)(2,1)}), bf16[128,1088]{1,0:T(8,128)(2,1)}) %reduce-scatter.21.cloned.1.call-update) | async-done | bytes 278544
  340.3 4.1 all-to-all-start.1
  344.4 6.0 convolution_convert_fusion.2
  350.5 4.2 copy.161
  366.3 4.7 fusion.11
  385.1 11.4 %collective-permute-done.1 = bf16[256,384]{0,1:T(8,128)(2,1)S(1)} collective-permute-done((bf16[256,384]{0,1:T(8,128)(2,1)S(1)}, bf16[256,384]{0,1:T(8,128)(2,1)S(1)}, u32[]{:S(2)}, u32[]{:S(2)}) %collective-permute-start.1) | collective-permute-done | bytes 196640 | tf_op jit(solution)/shard_map/ppermute | solution.py:18
  403.4 5.6 fusion.68
  409.0 4.3 copy.165
  414.2 34.5 %reduce-scatter.27.cloned.1.call-done = bf16[1,136,2176]{2,1,0:T(8,128)(2,1)} async-done(((bf16[4,136,2176]{2,1,0:T(8,128)(2,1)}), bf16[1,136,2176]{2,1,0:T(8,128)(2,1)}) %reduce-scatter.27.cloned.1.call-update) | async-done | bytes 591888
  449.4 45.2 %reduce-scatter.19.cloned.1.call-done = bf16[128,1088]{1,0:T(8,128)(2,1)} async-done(((bf16[1024,1088]{1,0:T(8,128)(2,1)}), bf16[128,1088]{1,0:T(8,128)(2,1)}) %reduce-scatter.19.cloned.1.call-update) | async-done | bytes 278544
  496.0 34.2 %reduce-scatter.17.cloned.1.call-done = bf16[1,272,576]{2,1,0:T(8,128)(2,1)} async-done(((bf16[4,272,576]{2,1,0:T(8,128)(2,1)}), bf16[1,272,576]{2,1,0:T(8,128)(2,1)}) %reduce-scatter.17.cloned.1.call-update) | async-done | bytes 313360 | tf_op jit(solution)/shard_map/reduce_scatter | solution.py:350
  534.0 6.0 all-to-all-done.2
  541.1 34.2 %reduce-scatter.23.cloned.1.call-done = bf16[128,1088]{1,0:T(8,128)(2,1)} async-done(((bf16[1024,1088]{1,0:T(8,128)(2,1)}), bf16[128,1088]{1,0:T(8,128)(2,1)}) %reduce-scatter.23.cloned.1.call-update) | async-done | bytes 278544
  578.4 39.9 %psum.15 = f32[13056]{0:T(1024)S(1)} all-reduce(f32[13056]{0:T(1024)S(1)} %concatenate.65), channel_id=1, replica_groups=mesh['shard'=4,'heads'=4,'tensor'=2] {'shard','heads','tensor'}, use_global_device_ids=true, to_apply=%region_31.32 | all-reduce | flops 13056 | bytes 104448 | tf_op jit(solution)/shard_map/psum | solution.py:402
  621.5 14.1 %all-gather.20.cloned.1.call-done = bf16[4,136,2176]{2,1,0:T(8,128)(2,1)} async-done(((bf16[1,136,2176]{2,1,0:T(8,128)(2,1)}), bf16[4,136,2176]{2,1,0:T(8,128)(2,1)}) %all-gather.20.cloned.1.call-update) | async-done | bytes 2367504 | tf_op jit(solution)/shard_map/all_gather | solution.py:306
  635.6 4.6 slice_convert_fusion
  640.2 16.1 %all-gather.26.cloned.1.call-done = bf16[8,136,576]{2,1,0:T(8,128)(2,1)} async-done(((bf16[2,136,576]{2,1,0:T(8,128)(2,1)}), bf16[8,136,576]{2,1,0:T(8,128)(2,1)}) %all-gather.26.cloned.1.call-update) | async-done | bytes 1253392 | tf_op jit(solution)/shard_map/all_gather | solution.py:365
  656.3 4.4 reshape.488
  (343 shorter events, 127.3 us)
Async XLA Ops:
  7.2 34.2 %all-gather.14.cloned.1.call-start = ((), (), s32[]{:S(2)}) async-start(), calls=%async_computation.9 | async-start | bytes 2506752 | tf_op jit(solution)/shard_map/all_gather | solution.py:207
  7.9 91.3 %all-gather.28.cloned.1.call-start = ((), (), s32[]{:S(2)}) async-start(), calls=%async_computation.18 | async-start | bytes 2985984 | tf_op jit(solution)/shard_map/all_gather | solution.py:208
  20.9 139.4 %all-gather.22.cloned.1.call-start = ((), (), s32[]{:S(2)}) async-start(), calls=%async_computation.15 | async-start | bytes 2820096 | tf_op jit(solution)/shard_map/all_gather | solution.py:244
  21.6 183.9 %all-gather.24.cloned.1.call-start = ((), (), s32[]{:S(2)}) async-start(), calls=%async_computation.16 | async-start | bytes 2959360 | tf_op jit(solution)/shard_map/all_gather | solution.py:252
  27.6 92.5 %copy-start.47 = (pred[3]{0:T(512)(128)(4,1)}, pred[3]{0:T(512)(128)(4,1)S(1)}, u32[]{:S(2)}) copy-start(pred[3]{0:T(512)(128)(4,1)S(1)} %iota_compare_fusion.2) | copy-start | bytes 13
  43.7 78.0 %copy-start.39 = (f32[1024]{0:T(1024)}, f32[1024]{0:T(1024)S(1)}, u32[]{:S(2)}) copy-start(f32[1024]{0:T(1024)S(1)} %broadcast_multiply_fusion) | copy-start | bytes 12292
  44.4 77.4 %copy-start.49 = (f32[1024]{0:T(1024)}, f32[1024]{0:T(1024)S(1)}, u32[]{:S(2)}) copy-start(f32[1024]{0:T(1024)S(1)} %add_rsqrt_fusion) | copy-start | bytes 12292
  124.8 11.9 %collective-permute-start = (bf16[256,384]{0,1:T(8,128)(2,1)S(1)}, bf16[256,384]{0,1:T(8,128)(2,1)S(1)}, u32[]{:S(2)}, u32[]{:S(2)}) collective-permute-start(bf16[256,384]{0,1:T(8,128)(2,1)S(1)} %slice.328), channel_id=1, source_target_pairs={{0,8},{8,16},{16,24},{1,9},{9,17},{17,25},{2,10},{10,18},{18,26},{... | collective-permute-start | bytes 589832 | tf_op jit(solution)/shard_map/ppermute | solution.py:18
  149.3 10.8 %all-to-all-start = ((bf16[8,128,192]{1,2,0:T(8,128)(2,1)}), bf16[8,128,192]{1,2,0:T(8,128)(2,1)S(1)}, u32[]{:S(2)}, u32[]{:S(2)}) async-start(bf16[8,128,192]{1,2,0:T(8,128)(2,1)} %copy_bitcast_fusion), calls=%async_computation | async-start | bytes 786432 | tf_op jit(solution)/shard_map/all_to_all | solution.py:116
  152.8 82.7 %all-gather.16.cloned.1.call-start = ((), (), s32[]{:S(2)}) async-start(), calls=%async_computation.10 | async-start | bytes 2506752 | tf_op jit(solution)/shard_map/all_gather | solution.py:288
  163.6 156.4 %copy-start.41 = (f32[128]{0:T(128)}, f32[128]{0:T(128)S(1)}, u32[]{:S(2)}) copy-start(f32[128]{0:T(128)S(1)} %fusion.63) | copy-start | bytes 1540
  164.7 95.8 %all-gather.18.cloned.1.call-start = ((), (), s32[]{:S(2)}) async-start(), calls=%async_computation.11 | async-start | bytes 2785280 | tf_op jit(solution)/shard_map/all_gather | solution.py:256
  165.3 152.1 %reduce-scatter.21.cloned.1.call-start = ((), (), s32[]{:S(2)}) async-start(), calls=%async_computation.20 | async-start | bytes 2654208
  274.7 138.7 %reduce-scatter.25.cloned.1.call-start = ((), (), s32[]{:S(2)}) async-start(), calls=%async_computation.22 | async-start | bytes 2820096
  323.7 124.9 %reduce-scatter.27.cloned.1.call-start = ((), (), s32[]{:S(2)}) async-start(), calls=%async_computation.23 | async-start | bytes 2959360
  340.3 14.7 %all-to-all-start.1 = ((bf16[8,128,192]{1,2,0:T(8,128)(2,1)}), bf16[8,128,192]{1,2,0:T(8,128)(2,1)}, u32[]{:S(2)}, u32[]{:S(2)}) async-start(bf16[8,128,192]{1,2,0:T(8,128)(2,1)} %bitcast_dynamic-update-slice_fusion), calls=%async_computation.1 | async-start | bytes 786432 | tf_op jit(solution)/shard_map/all_to_all | solution.py:116
  344.4 150.2 %reduce-scatter.19.cloned.1.call-start = ((), (), s32[]{:S(2)}) async-start(), calls=%async_computation.19 | async-start | bytes 2654208
  354.7 175.6 %reduce-scatter.17.cloned.1.call-start = ((), (), s32[]{:S(2)}) async-start(), calls=%async_computation.12 | async-start | bytes 1740800 | tf_op jit(solution)/shard_map/reduce_scatter | solution.py:350
  381.5 15.0 %collective-permute-start.1 = (bf16[256,384]{0,1:T(8,128)(2,1)S(1)}, bf16[256,384]{0,1:T(8,128)(2,1)S(1)}, u32[]{:S(2)}, u32[]{:S(2)}) collective-permute-start(bf16[256,384]{0,1:T(8,128)(2,1)S(1)} %pad_maximum_fusion.4), channel_id=1, source_target_pairs={{8,0},{16,8},{24,16},{9,1},{17,9},{25,17},{10,2},{18,10},{26,18},{... | collective-permute-start | bytes 589832 | tf_op jit(solution)/shard_map/ppermute | solution.py:18
  403.1 172.2 %reduce-scatter.23.cloned.1.call-start = ((), (), s32[]{:S(2)}) async-start(), calls=%async_computation.21 | async-start | bytes 2654208
  413.3 82.5 %copy-start.10 = (bf16[1024,384]{0,1:T(8,128)(2,1)S(1)}, bf16[1024,384]{0,1:T(8,128)(2,1)}, u32[]{:S(2)}) copy-start(bf16[1024,384]{0,1:T(8,128)(2,1)} %copy-done.9) | copy-start | bytes 2359300
  413.3 82.5 %copy-start.32 = (bf16[3,64,512]{2,1,0:T(8,128)(2,1)S(1)}, bf16[3,64,512]{2,1,0:T(8,128)(2,1)}, u32[]{:S(2)}) copy-start(bf16[3,64,512]{2,1,0:T(8,128)(2,1)} %copy-done.31) | copy-start | bytes 589828
  413.3 82.5 %copy-start.34 = (bf16[3,64,512]{2,1,0:T(8,128)(2,1)S(1)}, bf16[3,64,512]{2,1,0:T(8,128)(2,1)}, u32[]{:S(2)}) copy-start(bf16[3,64,512]{2,1,0:T(8,128)(2,1)} %copy-done.33) | copy-start | bytes 589828
  413.3 127.4 %copy-start.48 = (pred[3]{0:T(512)(128)(4,1)S(1)}, pred[3]{0:T(512)(128)(4,1)}, u32[]{:S(2)}) copy-start(pred[3]{0:T(512)(128)(4,1)} %copy-done.47) | copy-start | bytes 13
  413.4 206.2 %all-reduce.18.cloned.1.call-start = ((), (), s32[]{:S(2)}) async-start(), calls=%async_computation.13 | async-start | bytes 626688 | tf_op jit(solution)/shard_map/psum | solution.py:335
  414.1 221.5 %all-gather.20.cloned.1.call-start = ((), (), s32[]{:S(2)}) async-start(), calls=%async_computation.14 | async-start | bytes 2959360 | tf_op jit(solution)/shard_map/all_gather | solution.py:306
  448.7 128.1 %copy-start.14 = (bf16[256,1088]{0,1:T(8,128)(2,1)S(1)}, bf16[256,1088]{0,1:T(8,128)(2,1)}, u32[]{:S(2)}) copy-start(bf16[256,1088]{0,1:T(8,128)(2,1)} %param.19) | copy-start | bytes 1671172
  448.7 128.1 %copy-start.42 = (f32[128]{0:T(128)S(1)}, f32[128]{0:T(128)}, u32[]{:S(2)}) copy-start(f32[128]{0:T(128)} %copy-done.41) | copy-start | bytes 1540
  448.7 128.1 %copy-start.46 = (f32[128]{0:T(128)S(1)}, f32[128]{0:T(128)}, u32[]{:S(2)}) copy-start(f32[128]{0:T(128)} %copy-done.45) | copy-start | bytes 1540
  448.7 128.1 %copy-start.52 = (f32[128]{0:T(128)S(1)}, f32[128]{0:T(128)}, u32[]{:S(2)}) copy-start(f32[128]{0:T(128)} %copy-done.51) | copy-start | bytes 1540
  530.3 9.7 %all-to-all-start.2 = ((bf16[2,136,576]{2,1,0:T(8,128)(2,1)}), bf16[2,136,576]{2,1,0:T(8,128)(2,1)S(1)}, u32[]{:S(2)}, u32[]{:S(2)}) async-start(bf16[2,136,576]{2,1,0:T(8,128)(2,1)} %bitcast.283), calls=%async_computation.3 | async-start | bytes 696320 | tf_op jit(solution)/shard_map/all_to_all | solution.py:358
  533.8 122.5 %all-gather.26.cloned.1.call-start = ((), (), s32[]{:S(2)}) async-start(), calls=%async_computation.17 | async-start | bytes 1740800 | tf_op jit(solution)/shard_map/all_gather | solution.py:365
  (52 other events, 322.5 us)
Sparse Core Ops, SparseCore 0:
  9.9 31.4 all-gather.13
  44.2 55.0 all-gather.27
  101.4 52.1 all-gather.21
  155.6 49.9 all-gather.23
  207.8 27.5 all-gather.15
  236.9 23.5 all-gather.17
  274.9 42.4 reduce-scatter.20
  323.8 75.7 reduce-scatter.24
  402.6 46.0 reduce-scatter.26
  451.8 42.7 reduce-scatter.18
  497.6 32.6 reduce-scatter.16
  533.9 41.4 reduce-scatter.22
  577.7 32.0 all-reduce.17
  611.2 24.3 all-gather.19
  637.6 18.6 all-gather.25

commit v2 on v1

v2 whole, which is shorter than its diff:
```python
import functools

import jax
import jax.numpy as jnp
from jax import lax
from jax.experimental import pallas as pl
from jax.experimental.pallas import tpu as pltpu
from jax.sharding import PartitionSpec as P

NH = 17
HD = 64
SLOTS = 3
QUERY_BLOCK = 256


EPS = 1e-05
NEG = -1e30


def from_behind(value, axis, steps):
    count = lax.axis_size(axis)
    leading, last = (max(0, -steps), min(count, count - steps))
    return lax.ppermute(value, axis, [(source, source + steps) for source in range(leading, last)])


def layer_norm(values, gain_vec, shift_vec):
    center = values - jnp.mean(values, axis=-1, keepdims=True)
    spread = jnp.mean(center * center, axis=-1, keepdims=True)
    return center * lax.rsqrt(spread + EPS) * gain_vec + shift_vec


def gelu_tanh(values):
    return jax.nn.gelu(values, approximate=True)


def masked_scores(keys, queries, bounds_ref, first_query, prev_tok):
    scores = dot_nt(keys, queries) * HD ** (-0.5)
    local_query = first_query + lax.broadcasted_iota(jnp.int32, (1, scores.shape[1]), 1)
    local_key = lax.broadcasted_iota(jnp.int32, scores.shape, 0) - prev_tok
    start = jnp.where(local_query >= bounds_ref[0], bounds_ref[0], bounds_ref[1])
    allowed = (local_key >= start) & (local_key <= local_query)
    return jnp.where(allowed, scores, NEG)


def attend_kernel(prev_tok, bounds_ref, query_ref, key_ref, value_ref, out_ref, total_ref):
    group_tok = query_ref.shape[0]
    block = min(QUERY_BLOCK, group_tok)
    for first in range(0, group_tok, block):
        last_key = first + block + prev_tok
        results = []
        for slot in range(SLOTS):
            columns = slice(slot * HD, (slot + 1) * HD)
            scores = masked_scores(
                key_ref[:last_key, columns],
                query_ref[first : first + block, columns],
                bounds_ref,
                first,
                prev_tok,
            )
            row_max = jnp.max(scores, axis=0, keepdims=True)
            exp_scores = jnp.exp(scores - row_max)
            row_total = jnp.sum(exp_scores, axis=0, keepdims=True)
            weights = (exp_scores * (1.0 / row_total)).astype(jnp.bfloat16)
            results.append(dot_tn(value_ref[:last_key, columns], weights))
            total_ref[slot : slot + 1, first : first + block] = row_max + jnp.log(row_total)
        out_ref[first : first + block, :] = jnp.concatenate(results, axis=0).T.astype(out_ref.dtype)


def attend_back_kernel(
    prev_tok,
    bounds_ref,
    query_ref,
    key_ref,
    value_ref,
    d_ref,
    total_ref,
    query_grad_ref,
    key_grad_ref,
    value_grad_ref,
):
    group_tok = query_ref.shape[0]
    block = min(QUERY_BLOCK, group_tok)
    key_grad_ref[...] = jnp.zeros_like(key_grad_ref)
    value_grad_ref[...] = jnp.zeros_like(value_grad_ref)
    for first in range(0, group_tok, block):
        last_key = first + block + prev_tok
        query_grads, key_grads, value_grads = [], [], []
        for slot in range(SLOTS):
            columns = slice(slot * HD, (slot + 1) * HD)
            queries = query_ref[first : first + block, columns]
            d_part = d_ref[first : first + block, columns]
            keys = key_ref[:last_key, columns]
            scores = masked_scores(keys, queries, bounds_ref, first, prev_tok)
            probs = jnp.exp(scores - total_ref[slot : slot + 1, first : first + block])
            d_probs = dot_nt(value_ref[:last_key, columns], d_part)
            row_inner = jnp.sum(probs * d_probs, axis=0, keepdims=True)
            d_scores = (probs * (d_probs - row_inner)).astype(jnp.bfloat16)
            query_grads.append(dot_tn(keys, d_scores) * HD ** (-0.5))
            key_grads.append(
                jnp.dot(d_scores, queries, preferred_element_type=jnp.float32) * HD ** (-0.5)
            )
            value_grads.append(
                jnp.dot(probs.astype(jnp.bfloat16), d_part, preferred_element_type=jnp.float32)
            )
        query_grad_ref[first : first + block, :] = jnp.concatenate(query_grads, axis=0).T.astype(
            query_grad_ref.dtype
        )
        key_grad_ref[:last_key, :] += jnp.concatenate(key_grads, axis=1)
        value_grad_ref[:last_key, :] += jnp.concatenate(value_grads, axis=1)


def local_call(kernel, out_shape, inputs, flops):
    vmem = pl.BlockSpec(memory_space=pltpu.VMEM)
    return pl.pallas_call(
        kernel,
        out_shape=out_shape,
        in_specs=[pl.BlockSpec(memory_space=pltpu.SMEM)] + [vmem] * (len(inputs) - 1),
        out_specs=[vmem] * len(out_shape),
        compiler_params=pltpu.CompilerParams(vmem_limit_bytes=48 * 1024 * 1024),
        cost_estimate=pl.CostEstimate(flops=flops, bytes_accessed=4_000_000, transcendentals=0),
    )(*inputs)


def attend(query_flat, key_flat, value_flat, bounds, prev_tok):
    group_tok, columns = query_flat.shape
    return local_call(
        functools.partial(attend_kernel, prev_tok),
        [
            jax.ShapeDtypeStruct((group_tok, columns), jnp.bfloat16),
            jax.ShapeDtypeStruct((SLOTS, group_tok), jnp.float32),
        ],
        (bounds, query_flat, key_flat, value_flat),
        16 * group_tok * key_flat.shape[0] * columns,
    )


def attend_back(query_flat, key_flat, value_flat, d_flat, totals, bounds, prev_tok):
    group_tok, columns = query_flat.shape
    key_count = key_flat.shape[0]
    return local_call(
        functools.partial(attend_back_kernel, prev_tok),
        [
            jax.ShapeDtypeStruct((group_tok, columns), jnp.bfloat16),
            jax.ShapeDtypeStruct((key_count, columns), jnp.float32),
            jax.ShapeDtypeStruct((key_count, columns), jnp.float32),
        ],
        (bounds, query_flat, key_flat, value_flat, d_flat, totals),
        40 * group_tok * key_count * columns,
    )


TEAM = ("heads", "tensor")
OWNERS = ("shard", "tensor")


def set_bounds(group_total, tensor_total):
    base_count, extra_count = NH // group_total, NH % group_total
    firsts, counts = [], []
    next_head = 0
    for group_idx in range(group_total):
        group_size = base_count + (1 if group_idx < extra_count else 0)
        larger = -(-group_size // tensor_total)
        for tensor_pos in range(tensor_total):
            filled = max(0, min(larger, group_size - tensor_pos * larger))
            firsts.append(next_head)
            counts.append(filled)
            next_head += filled
    return firsts, counts


def swap(values, axes):
    return lax.all_to_all(values, axes, split_axis=0, concat_axis=0, tiled=True)


def gather_parts(values, axes):
    return swap(jnp.broadcast_to(values[None], (lax.axis_size(axes), *values.shape)), axes)


def sum_parts(values, axes):
    return jnp.sum(swap(values, axes).astype(jnp.float32), axis=0)


def team_sum(values):
    team = lax.axis_size(TEAM)
    rows = values.shape[0] // team
    return sum_parts(values.astype(jnp.bfloat16).reshape(team, rows, values.shape[1]), TEAM)


def dot_nt(left, right):
    return lax.dot_general(
        left, right, (((1,), (1,)), ((), ())), preferred_element_type=jnp.float32
    )


def dot_tn(left, right):
    return lax.dot_general(
        left, right, (((0,), (0,)), ((), ())), preferred_element_type=jnp.float32
    )


def shards(
    tokens,
    cotangent,
    cut_pos,
    attend_weight,
    out_weight,
    up_weight,
    down_weight,
    first_gain,
    first_bias,
    query_bias,
    value_bias,
    out_bias,
    second_gain,
    second_bias,
    up_bias,
    down_bias,
):
    tok_rows, width = tokens.shape
    heads_count = lax.axis_size("heads")
    tensor_count = lax.axis_size("tensor")
    shard_count = lax.axis_size("shard")
    team = heads_count * tensor_count
    group_tok = tok_rows * team
    prev_tok = group_tok // 4
    key_count = group_tok + prev_tok
    score_scale = HD ** (-0.5)
    slot_width = SLOTS * HD
    shard_idx = lax.axis_index("shard")
    heads_idx = lax.axis_index("heads")
    tensor_idx = lax.axis_index("tensor")
    set_idx = heads_idx * tensor_count + tensor_idx
    firsts, counts = set_bounds(heads_count, tensor_count)
    first_table = jnp.array(firsts, jnp.int32)
    count_table = jnp.array(counts, jnp.int32)
    my_first = first_table[set_idx]
    my_count = count_table[set_idx]
    column_valid = jnp.arange(slot_width) < my_count * HD
    group_first = first_table[heads_idx * tensor_count]
    group_span = max(
        sum(counts[g * tensor_count : (g + 1) * tensor_count]) for g in range(heads_count)
    )
    tail_heads = max(max(firsts) + SLOTS, max(firsts[::tensor_count]) + group_span, NH) - NH
    own_rows = attend_weight.shape[0]
    hidden_own = up_weight.shape[1]
    hidden_part = hidden_own // heads_count

    span = group_span * HD
    padded_weight = jnp.pad(attend_weight, ((0, 0), (0, tail_heads * HD)))
    packed = jnp.concatenate(
        [
            lax.dynamic_slice_in_dim(padded_weight, part * width + group_first * HD, span, 1)
            for part in range(3)
        ],
        axis=1,
    )
    vectors = jnp.concatenate(
        [
            first_gain,
            first_bias,
            query_bias,
            value_bias,
            out_bias,
            second_gain,
            second_bias,
            down_bias,
            up_bias,
        ]
    )
    token_all = gather_parts(tokens, TEAM).reshape(group_tok, width)
    packed_all = lax.all_gather(packed, OWNERS, axis=0, tiled=True)
    vector_all = gather_parts(vectors, OWNERS)
    (
        gain_one,
        shift_one,
        bias_query,
        bias_value,
        bias_out,
        gain_two,
        shift_two,
        bias_down,
    ) = (
        vector_all[:, member * own_rows : (member + 1) * own_rows]
        .reshape(width)
        .astype(jnp.float32)
        for member in range(8)
    )
    bias_up = vector_all[:, 8 * own_rows : 8 * own_rows + hidden_own].reshape(
        shard_count, tensor_count, heads_count, hidden_part
    )
    bias_up = lax.dynamic_slice(
        bias_up, (0, tensor_idx, heads_idx, 0), (shard_count, 1, 1, hidden_part)
    ).reshape(shard_count * hidden_part)
    packed_all = jnp.pad(packed_all, ((0, 0), (0, slot_width)))
    set_offset = (my_first - group_first) * HD
    w_set = jnp.concatenate(
        [
            jnp.where(
                column_valid,
                lax.dynamic_slice_in_dim(packed_all, part * span + set_offset, slot_width, 1),
                0,
            )
            for part in range(3)
        ],
        axis=1,
    )

    def set_vector(vector):
        padded = jnp.pad(vector, (0, tail_heads * HD))
        return jnp.where(
            column_valid, lax.dynamic_slice_in_dim(padded, my_first * HD, slot_width, 0), 0
        )

    bias_set = jnp.concatenate(
        [set_vector(bias_query), jnp.zeros((slot_width,), jnp.float32), set_vector(bias_value)]
    )
    out_cut = width // heads_count
    w_out = gather_parts(
        lax.all_gather(
            lax.dynamic_slice_in_dim(out_weight, heads_idx * out_cut, out_cut, 1),
            OWNERS,
            axis=0,
            tiled=True,
        ),
        "heads",
    )
    feed_part = jnp.concatenate(
        [
            lax.dynamic_slice_in_dim(up_weight, heads_idx * hidden_part, hidden_part, 1).T,
            lax.dynamic_slice_in_dim(down_weight, heads_idx * hidden_part, hidden_part, 0),
        ],
        axis=1,
    )
    feed_all = lax.all_gather(feed_part, "shard", axis=0, tiled=True)
    w_up, w_down = feed_all[:, :width], feed_all[:, width:]
    grad_all = gather_parts(cotangent, "heads").reshape(group_tok, width)

    token_f = token_all.astype(jnp.float32)
    center = token_f - jnp.mean(token_f, axis=-1, keepdims=True)
    inverse = lax.rsqrt(jnp.mean(center * center, axis=-1, keepdims=True) + EPS)
    unit = center * inverse
    normed = (unit * gain_one + shift_one).astype(jnp.bfloat16)
    projected = (
        jnp.dot(normed, w_set, preferred_element_type=jnp.float32) + bias_set
    ).astype(jnp.bfloat16)
    query_flat = projected[:, :slot_width]
    own_pair = projected[:, slot_width:]
    earlier = from_behind(own_pair[group_tok - prev_tok :], "shard", 1)
    pair_rows = jnp.concatenate([earlier, own_pair], axis=0)
    key_flat, value_flat = pair_rows[:, :slot_width], pair_rows[:, slot_width:]
    cut_here = cut_pos[shard_idx]
    cut_before = cut_pos[jnp.maximum(shard_idx - 1, 0)]
    earlier_start = jnp.where(shard_idx > 0, cut_before - group_tok, 0)
    bounds = jnp.stack([cut_here, earlier_start]).astype(jnp.int32)
    attended, log_totals = attend(query_flat, key_flat, value_flat, bounds, prev_tok)
    returned = swap(attended.reshape(team, tok_rows, slot_width), TEAM)
    attn_tok = jnp.concatenate(
        [returned[member, :, : counts[member] * HD] for member in range(team)], axis=1
    )
    own_tok_f = tokens.astype(jnp.float32)
    branch_f = jnp.concatenate(
        [
            jnp.dot(attn_tok, w_out[member], preferred_element_type=jnp.float32)
            for member in range(heads_count)
        ],
        axis=1,
    )
    resid = own_tok_f + branch_f + bias_out
    normed_two_f, norm_two_back = jax.vjp(layer_norm, resid, gain_two, shift_two)
    normed_two = normed_two_f.astype(jnp.bfloat16)

    own_grad_rows = lax.dynamic_slice_in_dim(cotangent, tensor_idx * tok_rows, tok_rows, 0)
    d_act = dot_nt(grad_all, w_down)
    feed_rows = gather_parts(normed_two, TEAM).reshape(group_tok, width)
    hidden_pre = dot_nt(feed_rows, w_up) + bias_up.astype(jnp.float32)
    hidden_act_f, gelu_back = jax.vjp(gelu_tanh, hidden_pre)
    hidden_act = hidden_act_f.astype(jnp.bfloat16)
    (d_pre_f,) = gelu_back(d_act)
    d_pre = d_pre_f.astype(jnp.bfloat16)
    d_normed_two = team_sum(jnp.dot(d_pre, w_up, preferred_element_type=jnp.float32))
    partial_out = jnp.dot(hidden_act, w_down, preferred_element_type=jnp.float32)
    fed_rows = team_sum(partial_out)
    layer_out = (resid + fed_rows + bias_down).astype(jnp.bfloat16)
    g_feed = jnp.concatenate([dot_tn(d_pre, feed_rows), dot_tn(hidden_act, grad_all)], axis=1)
    g_bias_up = jnp.sum(d_pre.astype(jnp.float32), axis=0)
    g_feed = sum_parts(
        g_feed.astype(jnp.bfloat16).reshape(shard_count, hidden_part, 2 * width), "shard"
    )
    g_feed = gather_parts(g_feed.astype(jnp.bfloat16), "heads").reshape(hidden_own, 2 * width)
    g_up = g_feed[:, :width].T.astype(jnp.float32)
    g_down = g_feed[:, width:].astype(jnp.float32)

    own_grad_f = own_grad_rows.astype(jnp.float32)
    g_bias_down = jnp.sum(own_grad_f, axis=0)
    d_resid_norm, g_gain_two, g_shift_two = norm_two_back(d_normed_two)
    d_resid = own_grad_f + d_resid_norm
    d_branch = d_resid.astype(jnp.bfloat16)
    g_bias_out = jnp.sum(d_branch.astype(jnp.float32), axis=0)
    d_attended = sum(
        dot_nt(d_branch[:, member * out_cut : (member + 1) * out_cut], w_out[member])
        for member in range(heads_count)
    ).astype(jnp.bfloat16)
    d_sets = jnp.stack(
        [
            jnp.pad(
                d_attended[:, firsts[member] * HD : (firsts[member] + counts[member]) * HD],
                ((0, 0), (0, slot_width - counts[member] * HD)),
            )
            for member in range(team)
        ],
        axis=0,
    )
    d_flat = swap(d_sets, TEAM).reshape(group_tok, slot_width)
    g_out = dot_tn(attn_tok, d_branch)
    g_out = sum_parts(
        g_out.astype(jnp.bfloat16).reshape(shard_count * tensor_count, own_rows, width), OWNERS
    )
    g_out = jnp.sum(
        gather_parts(g_out.astype(jnp.bfloat16), "heads").astype(jnp.float32), axis=0
    )

    query_grad, key_grad, value_grad = attend_back(
        query_flat, key_flat, value_flat, d_flat, log_totals, bounds, prev_tok
    )
    spill = jnp.concatenate([key_grad[:prev_tok], value_grad[:prev_tok]], axis=1)
    later = from_behind(spill.astype(jnp.bfloat16), "shard", -1).astype(jnp.float32)
    later = jnp.pad(later, ((group_tok - prev_tok, 0), (0, 0)))
    own_grads = jnp.concatenate([key_grad[prev_tok:], value_grad[prev_tok:]], axis=1) + later
    d_projected = jnp.concatenate(
        [query_grad.astype(jnp.bfloat16), own_grads.astype(jnp.bfloat16)], axis=1
    )
    d_normed_part = dot_nt(d_projected, w_set)
    d_normed = team_sum(d_normed_part)
    g_attend = dot_tn(normed, d_projected)
    g_attend = sum_parts(
        g_attend.astype(jnp.bfloat16).reshape(
            shard_count, tensor_count * own_rows, 3 * slot_width
        ),
        "shard",
    )
    g_attend = g_attend.astype(jnp.bfloat16).reshape(1, tensor_count, own_rows, 3 * slot_width)
    g_attend = swap(
        jnp.broadcast_to(g_attend, (heads_count, *g_attend.shape[1:])).reshape(
            team, own_rows, 3 * slot_width
        ),
        TEAM,
    )
    g_attend = jnp.concatenate(
        [
            g_attend[member, :, part * slot_width : part * slot_width + counts[member] * HD]
            for part in range(3)
            for member in range(team)
        ],
        axis=1,
    ).astype(jnp.float32)

    d_sum = jnp.sum(d_projected.astype(jnp.float32), axis=0)

    def place_vector(vector):
        spread = jnp.zeros((width + tail_heads * HD,), jnp.float32)
        own_terms = jnp.where(column_valid, vector, 0)
        return lax.dynamic_update_slice_in_dim(spread, own_terms, my_first * HD, 0)[:width]

    g_bias_up_all = lax.dynamic_update_slice(
        jnp.zeros((shard_count, tensor_count, heads_count, hidden_part), jnp.float32),
        g_bias_up.reshape(shard_count, 1, 1, hidden_part),
        (0, tensor_idx, heads_idx, 0),
    ).reshape(-1)
    owners = shard_count * tensor_count
    terms = jnp.concatenate(
        [
            vector.reshape(owners, -1)
            for vector in (
                jnp.sum(d_normed_part * unit, axis=0),
                jnp.sum(d_normed_part, axis=0),
                place_vector(d_sum[:slot_width]),
                place_vector(d_sum[2 * slot_width :]),
                g_bias_out,
                g_gain_two,
                g_shift_two,
                g_bias_down,
                g_bias_up_all,
            )
        ],
        axis=1,
    )
    sums = jnp.sum(gather_parts(sum_parts(terms, OWNERS), "heads"), axis=0)
    (
        s_gain_one,
        s_shift_one,
        s_bias_query,
        s_bias_value,
        s_bias_out,
        s_gain_two,
        s_shift_two,
        s_bias_down,
    ) = (sums[member * own_rows : (member + 1) * own_rows] for member in range(8))
    s_bias_up = sums[8 * own_rows :]

    own_center = own_tok_f - jnp.mean(own_tok_f, axis=-1, keepdims=True)
    own_inverse = lax.rsqrt(jnp.mean(own_center * own_center, axis=-1, keepdims=True) + EPS)
    own_unit = own_center * own_inverse
    scaled = d_normed * gain_one
    tokens_grad = d_resid + own_inverse * (
        scaled
        - jnp.mean(scaled, axis=-1, keepdims=True)
        - own_unit * jnp.mean(scaled * own_unit, axis=-1, keepdims=True)
    )
    return (
        layer_out,
        tokens_grad,
        g_attend,
        g_out,
        g_up,
        g_down,
        s_gain_one,
        s_shift_one,
        s_bias_query,
        s_bias_value,
        s_bias_out,
        s_gain_two,
        s_shift_two,
        s_bias_up,
        s_bias_down,
    )


def solution(mesh):
    placed = (
        P(("shard", "heads", "tensor"), None),
        P(("shard", "heads"), None),
        P(),
        P(("shard", "tensor"), None),
        P(("shard", "tensor"), None),
        P(None, ("shard", "tensor")),
        P(("shard", "tensor"), None),
        P(("shard", "tensor")),
        P(("shard", "tensor")),
        P(("shard", "tensor")),
        P(("shard", "tensor")),
        P(("shard", "tensor")),
        P(("shard", "tensor")),
        P(("shard", "tensor")),
        P(("shard", "tensor")),
        P(("shard", "tensor")),
    )
    return jax.shard_map(
        shards,
        mesh=mesh,
        in_specs=placed,
        out_specs=(
            P(("shard", "heads", "tensor"), None),
            P(("shard", "heads", "tensor"), None),
            P(("shard", "tensor"), None),
            P(("shard", "tensor"), None),
            P(None, ("shard", "tensor")),
            P(("shard", "tensor"), None),
            P(("shard", "tensor")),
            P(("shard", "tensor")),
            P(("shard", "tensor")),
            P(("shard", "tensor")),
            P(("shard", "tensor")),
            P(("shard", "tensor")),
            P(("shard", "tensor")),
            P(("shard", "tensor")),
            P(("shard", "tensor")),
        ),
        check_vma=False,
    )
```

time: 681 us -> 698 us (1.025)
  waiting for transfers between devices: 409 us -> 343 us
  starting transfers between devices: 18.1 us -> 71.4 us
  blocking collectives: 39.9 us -> 64 us
  Pallas kernels: 0 us -> 20.9 us
  matrix products: 65.9 us -> 45.4 us
    all_to_all x3 -> x16, waiting for transfers between devices: 13 us -> 329 us  [swap(): return lax.all_to_all(values, axes, split_axis=0, concat_axis=0, tiled=True)]
    all_gather x8 -> x2, waiting for transfers between devices: 183 us -> 6.64 us  [the longest x1 6.64 us: shards(): packed_all = lax.all_gather(packed, OWNERS, axis=0, tiled=True)]
    unnamed x20 -> x2, waiting for transfers between devices: 159 us -> 0.03 us
    all_to_all x3 -> x16, starting transfers between devices: 11 us -> 66 us  [swap(): return lax.all_to_all(values, axes, split_axis=0, concat_axis=0, tiled=True)]
    psum x1 -> x0, blocking collectives: 39.9 us -> none  [shards(): sums = lax.psum(terms, ('shard', 'heads', 'tensor'))]
    all_gather x0 -> x1, blocking collectives: none -> 39.7 us  [shards(): lax.all_gather(lax.dynamic_slice_in_dim(out_weight, heads_idx * out_cut,...]
    reduce_scatter x1 -> x0, waiting for transfers between devices: 34.2 us -> none  [shards(): lax.psum_scatter(g_attend.astype(jnp.bfloat16).reshape(shard_count, tenso...]
    unnamed x174 -> x103, local copies, waits for them, and re-layouts: 33.9 us -> 7.52 us
  transfers between devices with their start and end apart: 20 -> 20, of which waited for: 16 -> 17; matrix products, arithmetic and copies ran while one was open for 22% -> 19% of each run, Pallas kernels for 0% -> 1%
where the time goes in v2:
time: 698 us; the launch traced here: 689 us
  waiting for transfers between devices  343 us (49%)
  local copies, waits for them, and re-layouts  84.7 us (12%)
  starting transfers between devices  71.4 us (10%)
  blocking collectives  64 us (9%)
  matrix products  45.4 us (7%)
  other arithmetic  40 us (6%)
  Pallas kernels  20.9 us (3%)
  between operations  19.4 us (3%)
    all_to_all x16, waiting for transfers between devices, swap(): return lax.all_to_all(values, axes, split_axis=0, concat_axis=0, tiled=True)  329 us
    all_to_all x16, starting transfers between devices, swap(): return lax.all_to_all(values, axes, split_axis=0, concat_axis=0, tiled=True)  66 us
    all_gather x1, blocking collectives, shards(): lax.all_gather(lax.dynamic_slice_in_dim(out_weight, heads_idx * out_cut,...  39.7 us
    all_to_all x2, blocking collectives, swap(): return lax.all_to_all(values, axes, split_axis=0, concat_axis=0, tiled=True)  24.3 us
    pallas_call x2, Pallas kernels, local_call(): pl.pallas_call(kernel, out_shape=out_shape, in_specs=[pl.BlockSpec(memory...  20.9 us
    dot_general x7, matrix products, dot_nt(): lax.dot_general(left, right, (((1,), (1,)), ((), ())), preferred_element_...  20.5 us
    all_to_all x4, local copies, waits for them, and re-layouts, swap(): return lax.all_to_all(values, axes, split_axis=0, concat_axis=0, tiled=True)  18.3 us
  transfers between devices with their start and end apart: 20, of which 17 were waited for; matrix products, arithmetic and copies ran while one was open for 19% of the time, Pallas kernels for 1%

profile of v2, /device:TPU:0, one launch (start us, length us, event | category | flops | bytes accessed | tf_op | source)
XLA Modules:
  0.0 689.2 jit_solution(15153384195241889939)
XLA Ops:
  11.4 6.1 concatenate.45
  19.0 14.0 %all_to_all.99 = bf16[8,2,816]{2,1,0:T(2,128)(2,1)S(1)} all-to-all(bf16[8,2,816]{2,1,0:T(2,128)(2,1)S(1)} %reshape.315), channel_id=1, replica_groups=mesh['shard'=4,'heads'=4,'tensor'=2] {'shard','tensor'}, dimensions={0} | all-to-all | bytes 52224 | tf_op jit(solution)/shard_map/all_to_all | solution.py:172
  46.7 28.6 %all-to-all-done = bf16[8,128,1088]{1,2,0:T(8,128)(2,1)S(1)} async-done(((bf16[8,128,1088]{1,2,0:T(8,128)(2,1)}), bf16[8,128,1088]{1,2,0:T(8,128)(2,1)S(1)}, u32[]{:S(2)}, u32[]{:S(2)}) %all-to-all-start) | async-done | bytes 2228256 | tf_op jit(solution)/shard_map/all_to_all | solution.py:172
  78.8 6.6 all-gather.3.cloned.1.call-done
  95.2 39.7 %all_gather.10 = bf16[1088,272]{1,0:T(8,128)(2,1)S(1)} all-gather(bf16[136,272]{1,0:T(8,128)(2,1)S(1)} %copy-done.27), channel_id=1, replica_groups=mesh['shard'=4,'heads'=4,'tensor'=2] {'shard','tensor'}, dimensions={0}, use_global_device_ids=true | all-gather | bytes 665856 | tf_op jit(solution)/shard_map/all_gather | solution.py:319
  140.2 9.6 %shard_map.289 = (bf16[1024,192]{1,0:T(8,128)(2,1)S(1)}, f32[3,1024]{1,0:T(4,128)S(1)}) custom-call(s32[2]{0:T(128)S(1)} %pad_add_fusion.bounds_ref, bf16[1024,192]{1,0:T(8,128)(2,1)S(1)} %slice.344.query_ref, bf16[1280,192]{1,0:T(8,128)(2,1)S(1)} %get-tuple-element.74.key_ref, bf16[1280,192]{1,0:T(8,128)(2,1)S(1)} %get-tuple-element.73.value_ref), custom_call_target="tpu_custom_call" | custom-call | flops 4026531840 | bytes 4000000 | tf_op jit(solution)/shard_map/pallas_call | solution.py:114
  155.3 7.0 %all-to-all-done.2 = bf16[8,128,192]{1,2,0:T(8,128)(2,1)S(1)} async-done(((bf16[8,128,192]{1,2,0:T(8,128)(2,1)}), bf16[8,128,192]{1,2,0:T(8,128)(2,1)S(1)}, u32[]{:S(2)}, u32[]{:S(2)}) %all-to-all-start.2) | async-done | bytes 393248 | tf_op jit(solution)/shard_map/all_to_all | solution.py:172
  163.9 4.7 all-to-all-start.3
  173.4 25.3 %all-to-all-done.3 = bf16[4,1088,272]{1,2,0:T(8,128)(2,1)} async-done(((bf16[4,1088,272]{1,2,0:T(8,128)(2,1)}), bf16[4,1088,272]{1,2,0:T(8,128)(2,1)}, u32[]{:S(2)}, u32[]{:S(2)}) %all-to-all-start.3) | async-done | bytes 2367520 | tf_op jit(solution)/shard_map/all_to_all | solution.py:172
  200.2 4.9 all-to-all-start.6
  212.3 19.9 %all-to-all-done.6 = bf16[4,256,1088]{1,2,0:T(8,128)(2,1)} async-done(((bf16[4,256,1088]{1,2,0:T(8,128)(2,1)}), bf16[4,256,1088]{1,2,0:T(8,128)(2,1)}, u32[]{:S(2)}, u32[]{:S(2)}) %all-to-all-start.6) | async-done | bytes 2228256 | tf_op jit(solution)/shard_map/all_to_all | solution.py:172
  242.6 5.0 fusion.35
  247.6 17.9 %all-to-all-done.4 = bf16[8,128,1088]{1,2,0:T(8,128)(2,1)} async-done(((bf16[8,128,1088]{1,2,0:T(8,128)(2,1)}), bf16[8,128,1088]{1,2,0:T(8,128)(2,1)}, u32[]{:S(2)}, u32[]{:S(2)}) %all-to-all-start.4) | async-done | bytes 2228256 | tf_op jit(solution)/shard_map/all_to_all | solution.py:172
  265.5 6.8 convert_reduce_fusion.7
  280.4 4.6 fusion.27
  286.8 20.8 %all-to-all-done.7 = bf16[8,128,1088]{1,2,0:T(8,128)(2,1)} async-done(((bf16[8,128,1088]{1,2,0:T(8,128)(2,1)}), bf16[8,128,1088]{1,2,0:T(8,128)(2,1)}, u32[]{:S(2)}, u32[]{:S(2)}) %all-to-all-start.7) | async-done | bytes 2228256 | tf_op jit(solution)/shard_map/all_to_all | solution.py:172
  307.6 4.5 all-to-all-start.5
  315.5 23.8 %all-to-all-done.5 = bf16[8,128,1088]{1,2,0:T(8,128)(2,1)} async-done(((bf16[8,128,1088]{1,2,0:T(8,128)(2,1)}), bf16[8,128,1088]{1,2,0:T(8,128)(2,1)}, u32[]{:S(2)}, u32[]{:S(2)}) %all-to-all-start.5) | async-done | bytes 2228256 | tf_op jit(solution)/shard_map/all_to_all | solution.py:172
  349.2 10.3 %all_to_all.100 = bf16[8,128,192]{1,2,0:T(8,128)(2,1)S(1)} all-to-all(bf16[8,128,192]{1,2,0:T(8,128)(2,1)S(1)} %bitcast_dynamic-update-slice_fusion), channel_id=1, replica_groups=mesh['shard'=4,'heads'=4,'tensor'=2] {'heads','tensor'}, dimensions={0} | all-to-all | bytes 786432 | tf_op jit(solution)/shard_map/all_to_all | solution.py:172
  359.7 11.3 %shard_map.290 = (bf16[1024,192]{1,0:T(8,128)(2,1)S(1)}, f32[1280,192]{1,0:T(8,128)S(1)}, f32[1280,192]{1,0:T(8,128)S(1)}) custom-call(s32[2]{0:T(128)S(1)} %pad_add_fusion.bounds_ref, bf16[1024,192]{1,0:T(8,128)(2,1)S(1)} %slice.344.query_ref, bf16[1280,192]{1,0:T(8,128)(2,1)S(1)} %get-tuple-element.74.key_ref, ...), custom_call_target="tpu_custom_call" | custom-call | flops 10066329600 | bytes 4000000 | tf_op jit(solution)/shard_map/pallas_call | solution.py:114
  373.1 7.4 %collective-permute-done.1 = bf16[256,384]{1,0:T(8,128)(2,1)S(1)} collective-permute-done((bf16[256,384]{1,0:T(8,128)(2,1)S(1)}, bf16[256,384]{1,0:T(8,128)(2,1)S(1)}, u32[]{:S(2)}, u32[]{:S(2)}) %collective-permute-start.1) | collective-permute-done | bytes 196640 | tf_op jit(solution)/shard_map/ppermute | solution.py:23
  388.8 10.6 %copy.66 = bf16[4,256,1088]{1,0,2:T(4,128)(2,1)} copy(bf16[4,256,1088]{1,2,0:T(8,128)(2,1)} %all-to-all-done.6) | data formatting | bytes 4456448 | tf_op jit(solution)/shard_map/all_to_all | solution.py:172
  399.4 5.1 reshape.311
  404.5 6.9 copy.64
  411.4 4.7 reshape.310
  425.1 4.7 all-to-all-start.14
  435.8 48.9 %all-to-all-done.14 = bf16[4,136,2176]{2,1,0:T(8,128)(2,1)} async-done(((bf16[4,136,2176]{2,1,0:T(8,128)(2,1)}), bf16[4,136,2176]{2,1,0:T(8,128)(2,1)}, u32[]{:S(2)}, u32[]{:S(2)}) %all-to-all-start.14) | async-done | bytes 2367520 | tf_op jit(solution)/shard_map/all_to_all | solution.py:172
  499.0 31.9 %all-to-all-done.10 = bf16[4,272,576]{2,1,0:T(8,128)(2,1)S(1)} async-done(((bf16[4,272,576]{2,1,0:T(8,128)(2,1)}), bf16[4,272,576]{2,1,0:T(8,128)(2,1)S(1)}, u32[]{:S(2)}, u32[]{:S(2)}) %all-to-all-start.10) | async-done | bytes 1253408 | tf_op jit(solution)/shard_map/all_to_all | solution.py:172
  547.1 25.3 %all-to-all-done.15 = bf16[4,136,2176]{2,1,0:T(8,128)(2,1)S(1)} async-done(((bf16[4,136,2176]{2,1,0:T(8,128)(2,1)}), bf16[4,136,2176]{2,1,0:T(8,128)(2,1)S(1)}, u32[]{:S(2)}, u32[]{:S(2)}) %all-to-all-start.15) | async-done | bytes 2367520 | tf_op jit(solution)/shard_map/all_to_all | solution.py:172
  578.6 55.4 %all-to-all-done.12 = bf16[8,136,1088]{2,1,0:T(8,128)(2,1)} async-done(((bf16[8,136,1088]{2,1,0:T(8,128)(2,1)}), bf16[8,136,1088]{2,1,0:T(8,128)(2,1)}, u32[]{:S(2)}, u32[]{:S(2)}) %all-to-all-start.12) | async-done | bytes 2367520 | tf_op jit(solution)/shard_map/all_to_all | solution.py:172
  643.0 14.7 %all-to-all-done.11 = bf16[8,136,576]{2,1,0:T(8,128)(2,1)} async-done(((bf16[8,136,576]{2,1,0:T(8,128)(2,1)}), bf16[8,136,576]{2,1,0:T(8,128)(2,1)}, u32[]{:S(2)}, u32[]{:S(2)}) %all-to-all-start.11) | async-done | bytes 1253408 | tf_op jit(solution)/shard_map/all_to_all | solution.py:172
  673.3 6.5 all-to-all-done.13
  (261 shorter events, 176.5 us)
Async XLA Ops:
  7.2 31.2 %copy-start = (bf16[1088,544]{0,1:T(8,128)(2,1)S(1)}, bf16[1088,544]{0,1:T(8,128)(2,1)}, u32[]{:S(2)}) copy-start(bf16[1088,544]{0,1:T(8,128)(2,1)} %param.23) | copy-start | bytes 3551236
  7.2 25.8 %copy-start.4 = (bf16[128,1088]{0,1:T(8,128)(2,1)S(1)}, bf16[128,1088]{0,1:T(8,128)(2,1)}, u32[]{:S(2)}) copy-start(bf16[128,1088]{0,1:T(8,128)(2,1)} %param.18) | copy-start | bytes 835588
  7.2 78.2 %all-gather.3.cloned.1.call-start = ((), (), s32[]{:S(2)}) async-start(), calls=%async_computation.18 | async-start | bytes 2506752 | tf_op jit(solution)/shard_map/all_gather | solution.py:271
  34.7 40.6 %all-to-all-start = ((bf16[8,128,1088]{1,2,0:T(8,128)(2,1)}), bf16[8,128,1088]{1,2,0:T(8,128)(2,1)S(1)}, u32[]{:S(2)}, u32[]{:S(2)}) async-start(bf16[8,128,1088]{1,2,0:T(8,128)(2,1)} %broadcast_in_dim.45), calls=%async_computation | async-start | bytes 4456448 | tf_op jit(solution)/shard_map/all_to_all | solution.py:172
  38.3 204.3 %all-gather.5.cloned.1.call-start = ((), (), s32[]{:S(2)}) async-start(), calls=%async_computation.19 | async-start | bytes 2959360 | tf_op jit(solution)/shard_map/all_gather | solution.py:334
  45.4 30.7 %copy-start.28 = (bf16[8,1,1632]{2,0,1:T(8,128)(2,1)}, bf16[8,1,1632]{2,0,1:T(8,128)(2,1)S(1)}, u32[]{:S(2)}) copy-start(bf16[8,1,1632]{2,0,1:T(8,128)(2,1)S(1)} %copy.108) | copy-start | bytes 78340
  78.8 9.4 %copy-start.17 = (bf16[1024,1088]{0,1:T(8,128)(2,1)S(1)}, bf16[1024,1088]{0,1:T(8,128)(2,1)}, u32[]{:S(2)}) copy-start(bf16[1024,1088]{0,1:T(8,128)(2,1)} %add_convert_fusion) | copy-start | bytes 6684676
  90.6 44.6 %copy-start.39 = (s32[4]{0:T(128)S(1)}, s32[4]{0:T(128)}, u32[]{:S(2)}) copy-start(s32[4]{0:T(128)} %param.20) | copy-start | bytes 52
  91.6 48.2 %collective-permute-start = (bf16[256,384]{1,0:T(8,128)(2,1)S(1)}, bf16[256,384]{1,0:T(8,128)(2,1)S(1)}, u32[]{:S(2)}, u32[]{:S(2)}) collective-permute-start(bf16[256,384]{1,0:T(8,128)(2,1)S(1)} %slice.345), channel_id=1, source_target_pairs={{0,8},{8,16},{16,24},{1,9},{9,17},{17,25},{2,10},{10,18},{18,26},{... | collective-permute-start | bytes 589832 | tf_op jit(solution)/shard_map/ppermute | solution.py:23
  140.2 14.7 %copy-start.5 = (bf16[128,1088]{0,1:T(8,128)(2,1)S(1)}, bf16[128,1088]{0,1:T(8,128)(2,1)}, u32[]{:S(2)}) copy-start(bf16[128,1088]{0,1:T(8,128)(2,1)} %param.18) | copy-start | bytes 835588
  140.2 14.8 %copy-start.30 = (f32[8,136]{1,0:T(8,128)S(1)}, f32[8,136]{1,0:T(8,128)}, u32[]{:S(2)}) copy-start(f32[8,136]{1,0:T(8,128)} %get-tuple-element.91) | copy-start | bytes 13060
  140.2 14.9 %copy-start.29 = (f32[8,136]{1,0:T(8,128)S(1)}, f32[8,136]{1,0:T(8,128)}, u32[]{:S(2)}) copy-start(f32[8,136]{1,0:T(8,128)} %get-tuple-element.90) | copy-start | bytes 13060
  150.7 11.6 %all-to-all-start.2 = ((bf16[8,128,192]{1,2,0:T(8,128)(2,1)}), bf16[8,128,192]{1,2,0:T(8,128)(2,1)S(1)}, u32[]{:S(2)}, u32[]{:S(2)}) async-start(bf16[8,128,192]{1,2,0:T(8,128)(2,1)} %copy.62), calls=%async_computation.2 | async-start | bytes 786432 | tf_op jit(solution)/shard_map/all_to_all | solution.py:172
  155.0 56.1 %copy-start.35 = (f32[128]{0:T(128)}, f32[128]{0:T(128)S(1)}, u32[]{:S(2)}) copy-start(f32[128]{0:T(128)S(1)} %broadcast_multiply_fusion.3) | copy-start | bytes 1540
  163.9 34.8 %copy-start.14 = (bf16[256,1088]{0,1:T(8,128)(2,1)S(1)}, bf16[256,1088]{0,1:T(8,128)(2,1)}, u32[]{:S(2)}) copy-start(bf16[256,1088]{0,1:T(8,128)(2,1)} %param.19) | copy-start | bytes 1671172
  163.9 34.8 %all-to-all-start.3 = ((bf16[4,1088,272]{1,2,0:T(8,128)(2,1)}), bf16[4,1088,272]{1,2,0:T(8,128)(2,1)}, u32[]{:S(2)}, u32[]{:S(2)}) async-start(bf16[4,1088,272]{1,2,0:T(8,128)(2,1)} %broadcast_in_dim.50), calls=%async_computation.3 | async-start | bytes 5013504 | tf_op jit(solution)/shard_map/all_to_all | solution.py:172
  200.2 32.0 %all-to-all-start.6 = ((bf16[4,256,1088]{1,2,0:T(8,128)(2,1)}), bf16[4,256,1088]{1,2,0:T(8,128)(2,1)}, u32[]{:S(2)}, u32[]{:S(2)}) async-start(bf16[4,256,1088]{1,2,0:T(8,128)(2,1)} %broadcast_in_dim.52), calls=%async_computation.6 | async-start | bytes 4456448 | tf_op jit(solution)/shard_map/all_to_all | solution.py:172
  233.9 31.6 %all-to-all-start.4 = ((bf16[8,128,1088]{1,2,0:T(8,128)(2,1)}), bf16[8,128,1088]{1,2,0:T(8,128)(2,1)}, u32[]{:S(2)}, u32[]{:S(2)}) async-start(bf16[8,128,1088]{1,2,0:T(8,128)(2,1)} %broadcast_in_dim.51), calls=%async_computation.4 | async-start | bytes 4456448 | tf_op jit(solution)/shard_map/all_to_all | solution.py:172
  276.1 31.6 %all-to-all-start.7 = ((bf16[8,128,1088]{1,2,0:T(8,128)(2,1)}), bf16[8,128,1088]{1,2,0:T(8,128)(2,1)}, u32[]{:S(2)}, u32[]{:S(2)}) async-start(bf16[8,128,1088]{1,2,0:T(8,128)(2,1)} %bitcast.235), calls=%async_computation.7 | async-start | bytes 4456448 | tf_op jit(solution)/shard_map/all_to_all | solution.py:172
  307.6 31.7 %all-to-all-start.5 = ((bf16[8,128,1088]{1,2,0:T(8,128)(2,1)}), bf16[8,128,1088]{1,2,0:T(8,128)(2,1)}, u32[]{:S(2)}, u32[]{:S(2)}) async-start(bf16[8,128,1088]{1,2,0:T(8,128)(2,1)} %bitcast.233), calls=%async_computation.5 | async-start | bytes 4456448 | tf_op jit(solution)/shard_map/all_to_all | solution.py:172
  371.2 9.3 %collective-permute-start.1 = (bf16[256,384]{1,0:T(8,128)(2,1)S(1)}, bf16[256,384]{1,0:T(8,128)(2,1)S(1)}, u32[]{:S(2)}, u32[]{:S(2)}) collective-permute-start(bf16[256,384]{1,0:T(8,128)(2,1)S(1)} %pad_maximum_fusion.10), channel_id=1, source_target_pairs={{8,0},{16,8},{24,16},{9,1},{17,9},{25,17},{10,2},{18,10},{26,18},{... | collective-permute-start | bytes 589832 | tf_op jit(solution)/shard_map/ppermute | solution.py:23
  385.2 39.9 %all-to-all-start.9 = ((bf16[8,128,1088]{1,2,0:T(8,128)(2,1)}), bf16[8,128,1088]{1,2,0:T(8,128)(2,1)S(1)}, u32[]{:S(2)}, u32[]{:S(2)}) async-start(bf16[8,128,1088]{1,2,0:T(8,128)(2,1)} %bitcast.234), calls=%async_computation.9 | async-start | bytes 4456448 | tf_op jit(solution)/shard_map/all_to_all | solution.py:172
  425.1 59.5 %all-to-all-start.14 = ((bf16[4,136,2176]{2,1,0:T(8,128)(2,1)}), bf16[4,136,2176]{2,1,0:T(8,128)(2,1)}, u32[]{:S(2)}, u32[]{:S(2)}) async-start(bf16[4,136,2176]{2,1,0:T(8,128)(2,1)} %pad_maximum_fusion), calls=%async_computation.14 | async-start | bytes 4734976 | tf_op jit(solution)/shard_map/all_to_all | solution.py:172
  433.0 55.5 %copy-start.13 = (bf16[1024,384]{1,0:T(8,128)(2,1)S(1)}, bf16[1024,384]{1,0:T(8,128)(2,1)}, u32[]{:S(2)}) copy-start(bf16[1024,384]{1,0:T(8,128)(2,1)} %copy-done.12) | copy-start | bytes 2359300
  484.7 10.7 %all-to-all-start.16 = ((f32[8,1,1632]{2,1,0:T(1,128)}), f32[8,1,1632]{2,1,0:T(1,128)S(1)}, u32[]{:S(2)}, u32[]{:S(2)}) async-start(f32[8,1,1632]{2,1,0:T(1,128)} %all_to_all.78), calls=%async_computation.16 | async-start | bytes 106496 | tf_op jit(solution)/shard_map/all_to_all | solution.py:172
  495.4 35.5 %all-to-all-start.10 = ((bf16[4,272,576]{2,1,0:T(8,128)(2,1)}), bf16[4,272,576]{2,1,0:T(8,128)(2,1)S(1)}, u32[]{:S(2)}, u32[]{:S(2)}) async-start(bf16[4,272,576]{2,1,0:T(8,128)(2,1)} %bitcast.32), calls=%async_computation.10 | async-start | bytes 2785280 | tf_op jit(solution)/shard_map/all_to_all | solution.py:172
  531.5 7.1 %all-to-all-start.17 = ((f32[4,1,1632]{2,1,0:T(1,128)}), f32[4,1,1632]{2,1,0:T(1,128)S(1)}, u32[]{:S(2)}, u32[]{:S(2)}) async-start(f32[4,1,1632]{2,1,0:T(1,128)} %broadcast_in_dim.60), calls=%async_computation.17 | async-start | bytes 53248 | tf_op jit(solution)/shard_map/all_to_all | solution.py:172
  540.3 32.2 %all-to-all-start.15 = ((bf16[4,136,2176]{2,1,0:T(8,128)(2,1)}), bf16[4,136,2176]{2,1,0:T(8,128)(2,1)S(1)}, u32[]{:S(2)}, u32[]{:S(2)}) async-start(bf16[4,136,2176]{2,1,0:T(8,128)(2,1)} %broadcast_in_dim.58), calls=%async_computation.15 | async-start | bytes 4734976 | tf_op jit(solution)/shard_map/all_to_all | solution.py:172
  572.5 61.5 %all-to-all-start.12 = ((bf16[8,136,1088]{2,1,0:T(8,128)(2,1)}), bf16[8,136,1088]{2,1,0:T(8,128)(2,1)}, u32[]{:S(2)}, u32[]{:S(2)}) async-start(bf16[8,136,1088]{2,1,0:T(8,128)(2,1)} %bitcast.232), calls=%async_computation.12 | async-start | bytes 5013504 | tf_op jit(solution)/shard_map/all_to_all | solution.py:172
  635.1 22.5 %all-to-all-start.11 = ((bf16[8,136,576]{2,1,0:T(8,128)(2,1)}), bf16[8,136,576]{2,1,0:T(8,128)(2,1)}, u32[]{:S(2)}, u32[]{:S(2)}) async-start(bf16[8,136,576]{2,1,0:T(8,128)(2,1)} %bitcast.236), calls=%async_computation.11 | async-start | bytes 2785280 | tf_op jit(solution)/shard_map/all_to_all | solution.py:172
  658.8 21.0 %all-to-all-start.13 = ((bf16[4,136,1088]{2,1,0:T(8,128)(2,1)}), bf16[4,136,1088]{2,1,0:T(8,128)(2,1)}, u32[]{:S(2)}, u32[]{:S(2)}) async-start(bf16[4,136,1088]{2,1,0:T(8,128)(2,1)} %broadcast_in_dim.57), calls=%async_computation.13 | async-start | bytes 2506752 | tf_op jit(solution)/shard_map/all_to_all | solution.py:172
  669.4 12.8 %copy-start.1 = (bf16[1088,544]{0,1:T(8,128)(2,1)S(1)}, bf16[1088,544]{0,1:T(8,128)(2,1)}, u32[]{:S(2)}) copy-start(bf16[1088,544]{0,1:T(8,128)(2,1)} %param.23) | copy-start | bytes 3551236
  (31 other events, 129.6 us)
Sparse Core Ops, SparseCore 0:
  11.5 73.8 all-gather.2
  87.5 57.3 all-gather.4

commit v3 on v2

--- a/solution.py
+++ b/solution.py
@@ -314,16 +314,7 @@
     bias_set = jnp.concatenate(
         [set_vector(bias_query), jnp.zeros((slot_width,), jnp.float32), set_vector(bias_value)]
     )
-    out_cut = width // heads_count
-    w_out = gather_parts(
-        lax.all_gather(
-            lax.dynamic_slice_in_dim(out_weight, heads_idx * out_cut, out_cut, 1),
-            OWNERS,
-            axis=0,
-            tiled=True,
-        ),
-        "heads",
-    )
+    w_out = lax.all_gather(out_weight, OWNERS, axis=0, tiled=True)
     feed_part = jnp.concatenate(
         [
             lax.dynamic_slice_in_dim(up_weight, heads_idx * hidden_part, hidden_part, 1).T,
@@ -358,13 +349,7 @@
         [returned[member, :, : counts[member] * HD] for member in range(team)], axis=1
     )
     own_tok_f = tokens.astype(jnp.float32)
-    branch_f = jnp.concatenate(
-        [
-            jnp.dot(attn_tok, w_out[member], preferred_element_type=jnp.float32)
-            for member in range(heads_count)
-        ],
-        axis=1,
-    )
+    branch_f = jnp.dot(attn_tok, w_out, preferred_element_type=jnp.float32)
     resid = own_tok_f + branch_f + bias_out
     normed_two_f, norm_two_back = jax.vjp(layer_norm, resid, gain_two, shift_two)
     normed_two = normed_two_f.astype(jnp.bfloat16)
@@ -379,14 +364,19 @@
     d_pre = d_pre_f.astype(jnp.bfloat16)
     d_normed_two = team_sum(jnp.dot(d_pre, w_up, preferred_element_type=jnp.float32))
     partial_out = jnp.dot(hidden_act, w_down, preferred_element_type=jnp.float32)
-    fed_rows = team_sum(partial_out)
+    fed_rows = lax.psum_scatter(
+        partial_out.astype(jnp.bfloat16), TEAM, scatter_dimension=0, tiled=True
+    ).astype(jnp.float32)
     layer_out = (resid + fed_rows + bias_down).astype(jnp.bfloat16)
     g_feed = jnp.concatenate([dot_tn(d_pre, feed_rows), dot_tn(hidden_act, grad_all)], axis=1)
     g_bias_up = jnp.sum(d_pre.astype(jnp.float32), axis=0)
-    g_feed = sum_parts(
-        g_feed.astype(jnp.bfloat16).reshape(shard_count, hidden_part, 2 * width), "shard"
-    )
-    g_feed = gather_parts(g_feed.astype(jnp.bfloat16), "heads").reshape(hidden_own, 2 * width)
+    g_feed = lax.psum_scatter(
+        g_feed.astype(jnp.bfloat16).reshape(shard_count, hidden_part, 2 * width),
+        "shard",
+        scatter_dimension=0,
+        tiled=False,
+    )
+    g_feed = lax.all_gather(g_feed, "heads", axis=0, tiled=False).reshape(hidden_own, 2 * width)
     g_up = g_feed[:, :width].T.astype(jnp.float32)
     g_down = g_feed[:, width:].astype(jnp.float32)
 
@@ -396,10 +386,7 @@
     d_resid = own_grad_f + d_resid_norm
     d_branch = d_resid.astype(jnp.bfloat16)
     g_bias_out = jnp.sum(d_branch.astype(jnp.float32), axis=0)
-    d_attended = sum(
-        dot_nt(d_branch[:, member * out_cut : (member + 1) * out_cut], w_out[member])
-        for member in range(heads_count)
-    ).astype(jnp.bfloat16)
+    d_attended = dot_nt(d_branch, w_out).astype(jnp.bfloat16)
     d_sets = jnp.stack(
         [
             jnp.pad(
@@ -412,12 +399,13 @@
     )
     d_flat = swap(d_sets, TEAM).reshape(group_tok, slot_width)
     g_out = dot_tn(attn_tok, d_branch)
-    g_out = sum_parts(
-        g_out.astype(jnp.bfloat16).reshape(shard_count * tensor_count, own_rows, width), OWNERS
-    )
-    g_out = jnp.sum(
-        gather_parts(g_out.astype(jnp.bfloat16), "heads").astype(jnp.float32), axis=0
-    )
+    g_out = lax.psum_scatter(
+        g_out.astype(jnp.bfloat16).reshape(shard_count * tensor_count, own_rows, width),
+        OWNERS,
+        scatter_dimension=0,
+        tiled=False,
+    )
+    g_out = lax.psum(g_out, "heads").astype(jnp.float32)
 
     query_grad, key_grad, value_grad = attend_back(
         query_flat, key_flat, value_flat, d_flat, log_totals, bounds, prev_tok

time: 698 us -> 501 us (0.72)
  waiting for transfers between devices: 343 us -> 226 us
  blocking collectives: 64 us -> 14 us
  starting transfers between devices: 71.4 us -> 52.3 us
    all_to_all x16 -> x11, waiting for transfers between devices: 329 us -> 161 us  [swap(): return lax.all_to_all(values, axes, split_axis=0, concat_axis=0, tiled=True)]
    all_gather x1 -> x0, blocking collectives: 39.7 us -> none  [shards(): lax.all_gather(lax.dynamic_slice_in_dim(out_weight, heads_idx * out_cut,...]
    all_gather x1, waiting for transfers between devices: 0.01 us -> 27.2 us  [shards(): feed_all = lax.all_gather(feed_part, 'shard', axis=0, tiled=True)]
    all_to_all x16 -> x11, starting transfers between devices: 66 us -> 45.7 us  [swap(): return lax.all_to_all(values, axes, split_axis=0, concat_axis=0, tiled=True)]
    all_gather x0 -> x2, waiting for transfers between devices: none -> 12.7 us  [the longest x1 12.7 us: shards(): w_out = lax.all_gather(out_weight, OWNERS, axis=0, tiled=True)]
    all_to_all x2 -> x1, blocking collectives: 24.3 us -> 14 us  [swap(): return lax.all_to_all(values, axes, split_axis=0, concat_axis=0, tiled=True)]
    unnamed x2 -> x11, waiting for transfers between devices: 0.03 us -> 9.85 us
    dot_general x7 -> x4, matrix products: 20.5 us -> 16.5 us  [dot_nt(): lax.dot_general(left, right, (((1,), (1,)), ((), ())), preferred_element_...]
  transfers between devices with their start and end apart: 20 -> 21, of which waited for: 17 -> 15; matrix products, arithmetic and copies ran while one was open for 19% -> 26% of each run, Pallas kernels for 1% -> 4%
where the time goes in v3:
time: 501 us; the launch traced here: 494 us
  waiting for transfers between devices  226 us (45%)
  local copies, waits for them, and re-layouts  78.1 us (16%)
  starting transfers between devices  52.3 us (10%)
  other arithmetic  42.2 us (8%)
  matrix products  41.5 us (8%)
  Pallas kernels  21 us (4%)
  between operations  19.1 us (4%)
  blocking collectives  14 us (3%)
    all_to_all x11, waiting for transfers between devices, swap(): return lax.all_to_all(values, axes, split_axis=0, concat_axis=0, tiled=True)  161 us
    all_to_all x11, starting transfers between devices, swap(): return lax.all_to_all(values, axes, split_axis=0, concat_axis=0, tiled=True)  45.7 us
    all_gather x1, waiting for transfers between devices, shards(): feed_all = lax.all_gather(feed_part, 'shard', axis=0, tiled=True)  27.2 us
    pallas_call x2, Pallas kernels, local_call(): pl.pallas_call(kernel, out_shape=out_shape, in_specs=[pl.BlockSpec(memory...  21 us
    all_to_all x4, local copies, waits for them, and re-layouts, swap(): return lax.all_to_all(values, axes, split_axis=0, concat_axis=0, tiled=True)  18.3 us
    dot_general x4, matrix products, dot_nt(): lax.dot_general(left, right, (((1,), (1,)), ((), ())), preferred_element_...  16.5 us
    all_to_all x1, blocking collectives, swap(): return lax.all_to_all(values, axes, split_axis=0, concat_axis=0, tiled=True)  14 us
    unnamed x67, local copies, waits for them, and re-layouts  12.8 us
  transfers between devices with their start and end apart: 21, of which 15 were waited for; matrix products, arithmetic and copies ran while one was open for 26% of the time, Pallas kernels for 4%

profile of v3, /device:TPU:0, one launch (start us, length us, event | category | flops | bytes accessed | tf_op | source)
XLA Modules:
  0.0 493.8 jit_solution(1479210600934691479)
XLA Ops:
  11.4 6.1 %concatenate.42 = bf16[1632]{0:T(1024)(128)(2,1)S(1)} concatenate(bf16[136]{0:T(256)(128)(2,1)} %param.25, bf16[136]{0:T(256)(128)(2,1)} %param.26, bf16[136]{0:T(256)(128)(2,1)} %param.27, bf16[136]{0:T(256)(128)(2,1)} %param.28, bf16[136]{0:T(256)(128)(2,1)} %param.29, bf16[136]{0:T(256)(128)(2,1)} %param.30, bf16[136]{0:T(256)(128)(2,1)} %param.31, bf16[136]{0:T(256)(128)(2,1)} %param.33, ...), dimensions={0} | concatenate | bytes 6528 | tf_op jit(solution)/shard_map/concatenate | solution.py:257
  19.0 14.0 %all_to_all.69 = bf16[8,2,816]{2,1,0:T(2,128)(2,1)S(1)} all-to-all(bf16[8,2,816]{2,1,0:T(2,128)(2,1)S(1)} %reshape.312), channel_id=1, replica_groups=mesh['shard'=4,'heads'=4,'tensor'=2] {'shard','tensor'}, dimensions={0} | all-to-all | bytes 52224 | tf_op jit(solution)/shard_map/all_to_all | solution.py:172
  34.7 4.5 all-to-all-start
  46.7 29.5 %all-to-all-done = bf16[8,128,1088]{1,2,0:T(8,128)(2,1)} async-done(((bf16[8,128,1088]{1,2,0:T(8,128)(2,1)}), bf16[8,128,1088]{1,2,0:T(8,128)(2,1)}, u32[]{:S(2)}, u32[]{:S(2)}) %all-to-all-start) | async-done | bytes 2228256 | tf_op jit(solution)/shard_map/all_to_all | solution.py:172
  97.8 5.3 %collective-permute-done = bf16[256,384]{1,0:T(8,128)(2,1)S(1)} collective-permute-done((bf16[256,384]{1,0:T(8,128)(2,1)S(1)}, bf16[256,384]{1,0:T(8,128)(2,1)S(1)}, u32[]{:S(2)}, u32[]{:S(2)}) %collective-permute-start) | collective-permute-done | bytes 196640 | tf_op jit(solution)/shard_map/ppermute | solution.py:23
  103.5 9.6 %shard_map.289 = (bf16[1024,192]{1,0:T(8,128)(2,1)S(1)}, f32[3,1024]{1,0:T(4,128)S(1)}) custom-call(s32[2]{0:T(128)S(1)} %pad_add_fusion.bounds_ref, bf16[1024,192]{1,0:T(8,128)(2,1)S(1)} %slice.307.query_ref, bf16[1280,192]{1,0:T(8,128)(2,1)S(1)} %get-tuple-element.72.key_ref, bf16[1280,192]{1,0:T(8,128)(2,1)S(1)} %get-tuple-element.71.value_ref), custom_call_target="tpu_custom_call" | custom-call | flops 4026531840 | bytes 4000000 | tf_op jit(solution)/shard_map/pallas_call | solution.py:114
  119.8 6.9 %all-to-all-done.2 = bf16[8,128,192]{1,2,0:T(8,128)(2,1)S(1)} async-done(((bf16[8,128,192]{1,2,0:T(8,128)(2,1)}), bf16[8,128,192]{1,2,0:T(8,128)(2,1)S(1)}, u32[]{:S(2)}, u32[]{:S(2)}) %all-to-all-start.2) | async-done | bytes 393248 | tf_op jit(solution)/shard_map/all_to_all | solution.py:172
  128.2 4.5 all-to-all-start.4
  132.8 12.7 %all-gather.7.cloned.1.call-done = bf16[1088,1088]{1,0:T(8,128)(2,1)} async-done(((bf16[136,1088]{1,0:T(8,128)(2,1)}), bf16[1088,1088]{1,0:T(8,128)(2,1)}) %all-gather.7.cloned.1.call-update) | async-done | bytes 2367504 | tf_op jit(solution)/shard_map/all_gather | solution.py:317
  149.0 10.9 %all-to-all-done.4 = bf16[4,256,1088]{1,2,0:T(8,128)(2,1)} async-done(((bf16[4,256,1088]{1,2,0:T(8,128)(2,1)}), bf16[4,256,1088]{1,2,0:T(8,128)(2,1)}, u32[]{:S(2)}, u32[]{:S(2)}) %all-to-all-start.4) | async-done | bytes 2228256 | tf_op jit(solution)/shard_map/all_to_all | solution.py:172
  161.5 4.4 all-to-all-start.3
  169.7 27.2 %all-gather.9.cloned.1.call-done = bf16[544,2176]{1,0:T(8,128)(2,1)} async-done(((bf16[136,2176]{1,0:T(8,128)(2,1)}), bf16[544,2176]{1,0:T(8,128)(2,1)}) %all-gather.9.cloned.1.call-update) | async-done | bytes 2367504 | tf_op jit(solution)/shard_map/all_gather | solution.py:325
  196.9 5.0 %fusion.34 = f32[544,1024]{1,0:T(8,128)} fusion(bf16[1024,1088]{0,1:T(8,128)(2,1)} %bitcast.219, bf16[544,2176]{1,0:T(8,128)(2,1)} %all-gather.9.cloned.1.call-done), kind=kOutput, calls=%fused_computation.75 | convolution fusion | flops 1212153856 | bytes 5709824 | tf_op jit(solution)/shard_map/dot_general | solution.py:190
  201.9 6.6 %convert_reduce_fusion.5 = (f32[544]{0:T(1024)S(1)}, bf16[1024,544]{0,1:T(8,128)(2,1)}, f32[1024,544]{0,1:T(8,128)S(1)}) fusion(f32[544]{0:T(1024)S(1)} %reshape.301, f32[544,1024]{1,0:T(8,128)} %fusion.34, bf16[544,2176]{1,0:T(8,128)(2,1)} %all-gather.9.cloned.1.call-done, bf16[8,128,1088]{1,2,0:T(8,128)(2,1)} %all-to-all-done.3), kind=kOutput, calls=%fused_computation.58 | convolution fusion | flops 1224965632 | bytes 9056512 | tf_op jit(solution)/shard_map/dot_general | solution.py:190
  213.8 4.1 copy.67
  223.3 4.4 all-to-all-start.5
  228.1 33.1 %all-to-all-done.5 = bf16[8,128,1088]{1,2,0:T(8,128)(2,1)} async-done(((bf16[8,128,1088]{1,2,0:T(8,128)(2,1)}), bf16[8,128,1088]{1,2,0:T(8,128)(2,1)}, u32[]{:S(2)}, u32[]{:S(2)}) %all-to-all-start.5) | async-done | bytes 2228256 | tf_op jit(solution)/shard_map/all_to_all | solution.py:172
  263.7 7.7 %reduce-scatter.10.cloned.1.call-done = bf16[128,1088]{1,0:T(8,128)(2,1)} async-done(((bf16[1024,1088]{1,0:T(8,128)(2,1)}), bf16[128,1088]{1,0:T(8,128)(2,1)}) %reduce-scatter.10.cloned.1.call-update) | async-done | bytes 278544
  279.5 10.6 %copy.60 = bf16[4,256,1088]{1,0,2:T(4,128)(2,1)} copy(bf16[4,256,1088]{1,2,0:T(8,128)(2,1)} %all-to-all-done.4) | data formatting | bytes 4456448 | tf_op jit(solution)/shard_map/all_to_all | solution.py:172
  290.1 5.1 %reshape.304 = bf16[1024,1088,1]{0,1,2:T(8,128)(2,1)} reshape(bf16[4,256,1088]{1,0,2:T(4,128)(2,1)} %copy.60) | data formatting | bytes 4456448 | tf_op jit(solution)/shard_map/reshape | solution.py:327
  295.2 6.9 %copy.59 = bf16[8,128,1088]{1,0,2:T(8,128)(2,1)} copy(bf16[8,128,1088]{1,2,0:T(8,128)(2,1)} %all-to-all-done.3) | data formatting | bytes 4456448 | tf_op jit(solution)/shard_map/all_to_all | solution.py:172
  302.1 4.7 reshape.303
  332.6 11.4 %shard_map.290 = (bf16[1024,192]{1,0:T(8,128)(2,1)S(1)}, f32[1280,192]{1,0:T(8,128)S(1)}, f32[1280,192]{1,0:T(8,128)S(1)}) custom-call(s32[2]{0:T(128)S(1)} %pad_add_fusion.bounds_ref, bf16[1024,192]{1,0:T(8,128)(2,1)S(1)} %slice.307.query_ref, bf16[1280,192]{1,0:T(8,128)(2,1)S(1)} %get-tuple-element.72.key_ref, ...), custom_call_target="tpu_custom_call" | custom-call | flops 10066329600 | bytes 4000000 | tf_op jit(solution)/shard_map/pallas_call | solution.py:114
  345.9 7.2 %collective-permute-done.1 = bf16[256,384]{1,0:T(8,128)(2,1)S(1)} collective-permute-done((bf16[256,384]{1,0:T(8,128)(2,1)S(1)}, bf16[256,384]{1,0:T(8,128)(2,1)S(1)}, u32[]{:S(2)}, u32[]{:S(2)}) %collective-permute-start.1) | collective-permute-done | bytes 196640 | tf_op jit(solution)/shard_map/ppermute | solution.py:23
  359.2 4.5 all-to-all-start.7
  365.8 25.1 %all-to-all-done.7 = bf16[8,128,1088]{1,2,0:T(8,128)(2,1)} async-done(((bf16[8,128,1088]{1,2,0:T(8,128)(2,1)}), bf16[8,128,1088]{1,2,0:T(8,128)(2,1)}, u32[]{:S(2)}, u32[]{:S(2)}) %all-to-all-start.7) | async-done | bytes 2228256 | tf_op jit(solution)/shard_map/all_to_all | solution.py:172
  395.1 4.6 all-to-all-start.10
  400.5 4.7 convolution_convert_fusion.3
  407.7 5.1 %all-to-all-start.8 = ((bf16[4,272,576]{2,1,0:T(8,128)(2,1)}), bf16[4,272,576]{2,1,0:T(8,128)(2,1)S(1)}, u32[]{:S(2)}, u32[]{:S(2)}) async-start(bf16[4,272,576]{2,1,0:T(8,128)(2,1)} %bitcast.217), calls=%async_computation.8 | async-start | bytes 2785280 | tf_op jit(solution)/shard_map/all_to_all | solution.py:172
  413.6 31.6 %all-to-all-done.8 = bf16[4,272,576]{2,1,0:T(8,128)(2,1)S(1)} async-done(((bf16[4,272,576]{2,1,0:T(8,128)(2,1)}), bf16[4,272,576]{2,1,0:T(8,128)(2,1)S(1)}, u32[]{:S(2)}, u32[]{:S(2)}) %all-to-all-start.8) | async-done | bytes 1253408 | tf_op jit(solution)/shard_map/all_to_all | solution.py:172
  459.3 16.8 %all-to-all-done.9 = bf16[8,136,576]{2,1,0:T(8,128)(2,1)S(1)} async-done(((bf16[8,136,576]{2,1,0:T(8,128)(2,1)}), bf16[8,136,576]{2,1,0:T(8,128)(2,1)S(1)}, u32[]{:S(2)}, u32[]{:S(2)}) %all-to-all-start.9) | async-done | bytes 1253408 | tf_op jit(solution)/shard_map/all_to_all | solution.py:172
  482.1 4.7 slice_convert_fusion
  (216 shorter events, 135.4 us)
Async XLA Ops:
  7.2 38.0 %copy-start = (bf16[1088,544]{0,1:T(8,128)(2,1)S(1)}, bf16[1088,544]{0,1:T(8,128)(2,1)}, u32[]{:S(2)}) copy-start(bf16[1088,544]{0,1:T(8,128)(2,1)} %param.23) | copy-start | bytes 3551236
  7.2 25.8 %copy-start.2 = (bf16[128,1088]{0,1:T(8,128)(2,1)S(1)}, bf16[128,1088]{0,1:T(8,128)(2,1)}, u32[]{:S(2)}) copy-start(bf16[128,1088]{0,1:T(8,128)(2,1)} %param.18) | copy-start | bytes 835588
  7.2 79.1 %all-gather.5.cloned.1.call-start = ((), (), s32[]{:S(2)}) async-start(), calls=%async_computation.15 | async-start | bytes 2506752 | tf_op jit(solution)/shard_map/all_gather | solution.py:271
  34.7 8.5 %copy-start.21 = (s32[4]{0:T(128)S(1)}, s32[4]{0:T(128)}, u32[]{:S(2)}) copy-start(s32[4]{0:T(128)} %param.20) | copy-start | bytes 52
  34.7 41.5 %all-to-all-start = ((bf16[8,128,1088]{1,2,0:T(8,128)(2,1)}), bf16[8,128,1088]{1,2,0:T(8,128)(2,1)}, u32[]{:S(2)}, u32[]{:S(2)}) async-start(bf16[8,128,1088]{1,2,0:T(8,128)(2,1)} %broadcast_in_dim.39), calls=%async_computation | async-start | bytes 4456448 | tf_op jit(solution)/shard_map/all_to_all | solution.py:172
  39.2 106.4 %all-gather.7.cloned.1.call-start = ((), (), s32[]{:S(2)}) async-start(), calls=%async_computation.16 | async-start | bytes 2820096 | tf_op jit(solution)/shard_map/all_gather | solution.py:317
  91.7 11.5 %collective-permute-start = (bf16[256,384]{1,0:T(8,128)(2,1)S(1)}, bf16[256,384]{1,0:T(8,128)(2,1)S(1)}, u32[]{:S(2)}, u32[]{:S(2)}) collective-permute-start(bf16[256,384]{1,0:T(8,128)(2,1)S(1)} %slice.308), channel_id=1, source_target_pairs={{0,8},{8,16},{16,24},{1,9},{9,17},{17,25},{2,10},{10,18},{18,26},{... | collective-permute-start | bytes 589832 | tf_op jit(solution)/shard_map/ppermute | solution.py:23
  113.0 13.7 %copy-start.7 = (bf16[256,1088]{0,1:T(8,128)(2,1)S(1)}, bf16[256,1088]{0,1:T(8,128)(2,1)}, u32[]{:S(2)}) copy-start(bf16[256,1088]{0,1:T(8,128)(2,1)} %param.19) | copy-start | bytes 1671172
  114.0 12.7 %all-to-all-start.2 = ((bf16[8,128,192]{1,2,0:T(8,128)(2,1)}), bf16[8,128,192]{1,2,0:T(8,128)(2,1)S(1)}, u32[]{:S(2)}, u32[]{:S(2)}) async-start(bf16[8,128,192]{1,2,0:T(8,128)(2,1)} %copy.58), calls=%async_computation.2 | async-start | bytes 786432 | tf_op jit(solution)/shard_map/all_to_all | solution.py:172
  117.5 79.4 %all-gather.9.cloned.1.call-start = ((), (), s32[]{:S(2)}) async-start(), calls=%async_computation.17 | async-start | bytes 2959360 | tf_op jit(solution)/shard_map/all_gather | solution.py:325
  128.2 31.7 %all-to-all-start.4 = ((bf16[4,256,1088]{1,2,0:T(8,128)(2,1)}), bf16[4,256,1088]{1,2,0:T(8,128)(2,1)}, u32[]{:S(2)}, u32[]{:S(2)}) async-start(bf16[4,256,1088]{1,2,0:T(8,128)(2,1)} %broadcast_in_dim.45), calls=%async_computation.4 | async-start | bytes 4456448 | tf_op jit(solution)/shard_map/all_to_all | solution.py:172
  132.8 16.1 %copy-start.13 = (bf16[128,1088]{0,1:T(8,128)(2,1)}, bf16[128,1088]{0,1:T(8,128)(2,1)S(1)}, u32[]{:S(2)}) copy-start(bf16[128,1088]{0,1:T(8,128)(2,1)S(1)} %constant_dynamic-update-slice_fusion) | copy-start | bytes 835588
  161.5 40.4 %all-to-all-start.3 = ((bf16[8,128,1088]{1,2,0:T(8,128)(2,1)}), bf16[8,128,1088]{1,2,0:T(8,128)(2,1)}, u32[]{:S(2)}, u32[]{:S(2)}) async-start(bf16[8,128,1088]{1,2,0:T(8,128)(2,1)} %broadcast_in_dim.44), calls=%async_computation.3 | async-start | bytes 4456448 | tf_op jit(solution)/shard_map/all_to_all | solution.py:172
  165.9 105.5 %reduce-scatter.10.cloned.1.call-start = ((), (), s32[]{:S(2)}) async-start(), calls=%async_computation.20 | async-start | bytes 2654208
  201.9 7.9 %copy-start.22 = (bf16[544,2176]{1,0:T(8,128)(2,1)S(1)}, bf16[544,2176]{1,0:T(8,128)(2,1)}, u32[]{:S(2)}) copy-start(bf16[544,2176]{1,0:T(8,128)(2,1)} %all-gather.9.cloned.1.call-done) | copy-start | bytes 7102468
  223.3 37.9 %all-to-all-start.5 = ((bf16[8,128,1088]{1,2,0:T(8,128)(2,1)}), bf16[8,128,1088]{1,2,0:T(8,128)(2,1)}, u32[]{:S(2)}, u32[]{:S(2)}) async-start(bf16[8,128,1088]{1,2,0:T(8,128)(2,1)} %bitcast.216), calls=%async_computation.5 | async-start | bytes 4456448 | tf_op jit(solution)/shard_map/all_to_all | solution.py:172
  227.7 172.1 %reduce-scatter.12.cloned.1.call-start = ((), (), s32[]{:S(2)}) async-start(), calls=%async_computation.21 | async-start | bytes 2820096
  263.7 13.6 %copy-start.14 = (bf16[128,1088]{0,1:T(8,128)(2,1)S(1)}, bf16[128,1088]{0,1:T(8,128)(2,1)}, u32[]{:S(2)}) copy-start(bf16[128,1088]{0,1:T(8,128)(2,1)} %copy-done.13) | copy-start | bytes 835588
  321.6 10.8 %all-to-all-start.6 = ((bf16[8,128,192]{1,2,0:T(8,128)(2,1)}), bf16[8,128,192]{1,2,0:T(8,128)(2,1)S(1)}, u32[]{:S(2)}, u32[]{:S(2)}) async-start(bf16[8,128,192]{1,2,0:T(8,128)(2,1)} %bitcast_dynamic-update-slice_fusion), calls=%async_computation.6 | async-start | bytes 786432 | tf_op jit(solution)/shard_map/all_to_all | solution.py:172
  325.1 87.7 %reduce-scatter.14.cloned.1.call-start = ((), (), s32[]{:S(2)}) async-start(), calls=%async_computation.22 | async-start | bytes 2959360
  344.2 8.8 %collective-permute-start.1 = (bf16[256,384]{1,0:T(8,128)(2,1)S(1)}, bf16[256,384]{1,0:T(8,128)(2,1)S(1)}, u32[]{:S(2)}, u32[]{:S(2)}) collective-permute-start(bf16[256,384]{1,0:T(8,128)(2,1)S(1)} %pad_maximum_fusion.10), channel_id=1, source_target_pairs={{8,0},{16,8},{24,16},{9,1},{17,9},{25,17},{10,2},{18,10},{26,18},{... | collective-permute-start | bytes 589832 | tf_op jit(solution)/shard_map/ppermute | solution.py:23
  345.8 7.6 %copy-start.16 = (bf16[1088,192]{1,0:T(8,128)(2,1)S(1)}, bf16[1088,192]{1,0:T(8,128)(2,1)}, u32[]{:S(2)}) copy-start(bf16[1088,192]{1,0:T(8,128)(2,1)} %copy-done.15) | copy-start | bytes 1253380
  345.8 7.6 %copy-start.18 = (bf16[1088,192]{1,0:T(8,128)(2,1)S(1)}, bf16[1088,192]{1,0:T(8,128)(2,1)}, u32[]{:S(2)}) copy-start(bf16[1088,192]{1,0:T(8,128)(2,1)} %copy-done.17) | copy-start | bytes 1253380
  359.2 31.7 %all-to-all-start.7 = ((bf16[8,128,1088]{1,2,0:T(8,128)(2,1)}), bf16[8,128,1088]{1,2,0:T(8,128)(2,1)}, u32[]{:S(2)}, u32[]{:S(2)}) async-start(bf16[8,128,1088]{1,2,0:T(8,128)(2,1)} %bitcast.215), calls=%async_computation.7 | async-start | bytes 4456448 | tf_op jit(solution)/shard_map/all_to_all | solution.py:172
  364.6 28.6 %copy-start.5 = (f32[128,1088]{0,1:T(8,128)S(1)}, f32[128,1088]{0,1:T(8,128)}, u32[]{:S(2)}) copy-start(f32[128,1088]{0,1:T(8,128)} %copy-done.4) | copy-start | bytes 1671172
  364.6 28.6 %copy-start.8 = (bf16[256,1088]{0,1:T(8,128)(2,1)S(1)}, bf16[256,1088]{0,1:T(8,128)(2,1)}, u32[]{:S(2)}) copy-start(bf16[256,1088]{0,1:T(8,128)(2,1)} %param.19) | copy-start | bytes 1671172
  395.1 12.6 %all-to-all-start.10 = ((f32[8,1,1632]{2,1,0:T(1,128)}), f32[8,1,1632]{2,1,0:T(1,128)S(1)}, u32[]{:S(2)}, u32[]{:S(2)}) async-start(f32[8,1,1632]{2,1,0:T(1,128)} %all_to_all.54), calls=%async_computation.10 | async-start | bytes 106496 | tf_op jit(solution)/shard_map/all_to_all | solution.py:172
  399.8 80.5 %all-reduce.16.cloned.1.call-start = ((), (), s32[]{:S(2)}) async-start(), calls=%async_computation.18 | async-start | bytes 626688 | tf_op jit(solution)/shard_map/psum | solution.py:408
  407.7 37.4 %all-to-all-start.8 = ((bf16[4,272,576]{2,1,0:T(8,128)(2,1)}), bf16[4,272,576]{2,1,0:T(8,128)(2,1)S(1)}, u32[]{:S(2)}, u32[]{:S(2)}) async-start(bf16[4,272,576]{2,1,0:T(8,128)(2,1)} %bitcast.217), calls=%async_computation.8 | async-start | bytes 2785280 | tf_op jit(solution)/shard_map/all_to_all | solution.py:172
  412.8 69.3 %all-gather.11.cloned.1.call-start = ((), (), s32[]{:S(2)}) async-start(), calls=%async_computation.19 | async-start | bytes 2959360 | tf_op jit(solution)/shard_map/all_gather | solution.py:379
  445.8 7.4 %all-to-all-start.11 = ((f32[4,1,1632]{2,1,0:T(1,128)}), f32[4,1,1632]{2,1,0:T(1,128)S(1)}, u32[]{:S(2)}, u32[]{:S(2)}) async-start(f32[4,1,1632]{2,1,0:T(1,128)} %broadcast_in_dim.95), calls=%async_computation.11 | async-start | bytes 53248 | tf_op jit(solution)/shard_map/all_to_all | solution.py:172
  454.4 21.7 %all-to-all-start.9 = ((bf16[8,136,576]{2,1,0:T(8,128)(2,1)}), bf16[8,136,576]{2,1,0:T(8,128)(2,1)S(1)}, u32[]{:S(2)}, u32[]{:S(2)}) async-start(bf16[8,136,576]{2,1,0:T(8,128)(2,1)} %bitcast.30), calls=%async_computation.9 | async-start | bytes 2785280 | tf_op jit(solution)/shard_map/all_to_all | solution.py:172
  (13 other events, 45.1 us)
Sparse Core Ops, SparseCore 0:
  11.5 74.7 all-gather.4
  88.5 57.0 all-gather.6
  147.7 49.1 all-gather.8
  218.1 53.2 reduce-scatter.9
  279.6 70.0 reduce-scatter.11
  352.6 46.3 reduce-scatter.13
  403.0 32.4 all-reduce.15
  437.0 24.5 all-gather.10
